TPU v7x, 256 devices: a whole 4x4x8 slice. The times are simulated.
256 devices in a mesh: row: 32 (over z, x), col: 8 (over y, core).
Axes of the slice: x: 4, y: 4, z: 8, core: 2. Of those that a mesh axis runs over, the one named last changes fastest.
Arguments:
- head_start: bfloat16 [512, 1024, 128], P('row', 'col'), may hold values from -6 to 6
- cotangent: bfloat16 [512, 1024, 128], P('row', 'col'), may hold values from -6 to 6
- conductivity: bfloat16 [512, 1024, 128], P('row', 'col'), may hold values from 0.19921875 to 2
- line_x: bfloat16 [512, 512], replicated, may hold values from -1 to 1.5
- line_y: bfloat16 [1024, 1024], replicated, may hold values from -1 to 1.5
- line_z: bfloat16 [128, 128], replicated, may hold values from -1 to 1.5
- zone_map: int32 [512, 1024], replicated, may hold values from 0 to 2047
- owner_order: int32 [2048], replicated, may hold values from 0 to 2047, each once
Outputs:
- head_adjoint: bfloat16 [512, 1024, 128], P('row', 'col')
- zone_grad: float32 [2048], P(('row', 'col'))
All inputs are finite; a program needn't handle non-finite values.
Results may differ from a plain program's by a relative error of at most 0.007.
Values may be sent and summed in bfloat16 or wider, within the bound.
A program may use at most 64 MiB of HBM per device.

v0:
```python
import math

import jax
import jax.numpy as jnp
from jax import lax
from jax.sharding import PartitionSpec as P

STEPS = 2


time_step = 0.15


def pad_side(values, direction, before):
    widths = [(0, 0)] * values.ndim
    widths[direction] = (before, 1 - before)
    return jnp.pad(values, widths)


def flux_divergence(heads, conduct, direction):
    length = heads.shape[direction]
    deltas = jnp.diff(heads, axis=direction)
    face_cond = 0.5 * (
        lax.slice_in_dim(conduct, 0, length - 1, axis=direction)
        + lax.slice_in_dim(conduct, 1, length, axis=direction)
    )
    fluxes = face_cond * deltas
    return pad_side(fluxes, direction, 0) - pad_side(fluxes, direction, 1)


def flux_product(states, backed, direction):
    products = jnp.diff(states, axis=direction) * jnp.diff(backed, axis=direction)
    return -0.5 * time_step * (pad_side(products, direction, 0) + pad_side(products, direction, 1))


def line_apply(matrix, source, direction, transpose):
    length = matrix.shape[0]
    if direction == 0:
        flattened = source.reshape(length, -1)
        contract = 0 if transpose else 1
        result = lax.dot_general(
            matrix, flattened, (((contract,), (0,)), ((), ())), preferred_element_type=jnp.float32
        )
        return result.reshape(source.shape)
    if direction == 1:
        pattern = "ji,ajb->aib" if transpose else "ij,ajb->aib"
        return jnp.einsum(pattern, matrix, source, preferred_element_type=jnp.float32)
    flattened = source.reshape(-1, length)
    contract = 0 if transpose else 1
    result = lax.dot_general(
        flattened, matrix, (((1,), (contract,)), ((), ())), preferred_element_type=jnp.float32
    )
    return result.reshape(source.shape)


def to_lines(heads, direction):
    if direction == 0:
        return lax.all_to_all(heads, "row", split_axis=1, concat_axis=0, tiled=True)
    if direction == 1:
        return lax.all_to_all(heads, "col", split_axis=0, concat_axis=1, tiled=True)
    return heads


def from_lines(heads, direction):
    if direction == 0:
        return lax.all_to_all(heads, "row", split_axis=0, concat_axis=1, tiled=True)
    if direction == 1:
        return lax.all_to_all(heads, "col", split_axis=1, concat_axis=0, tiled=True)
    return heads


def pair_to_lines(adjoint, states, direction):
    if direction == 0:
        return (
            lax.all_to_all(adjoint, "row", split_axis=1, concat_axis=0, tiled=True),
            lax.all_to_all(states, "row", split_axis=1, concat_axis=0, tiled=True),
        )
    if direction == 1:
        return (
            lax.all_to_all(adjoint, "col", split_axis=0, concat_axis=1, tiled=True),
            lax.all_to_all(states, "col", split_axis=0, concat_axis=1, tiled=True),
        )
    return (adjoint, states)


def on_device(head_start, cotangent, conductivity, line_x, line_y, line_z, zone_map, owner_order):
    row_index = lax.axis_index("row")
    col_index = lax.axis_index("col")
    row_count = lax.axis_size("row")
    col_count = lax.axis_size("col")
    slab_x, slab_y, depth_cells = head_start.shape
    part_y = slab_y // row_count
    part_x = slab_x // col_count
    total_x, total_y = zone_map.shape
    zone_count = owner_order.shape[0]
    conduct_rows = lax.all_to_all(
        conductivity, "row", split_axis=1, concat_axis=0, tiled=True
    ).astype(jnp.float32)
    conduct_cols = lax.all_to_all(
        conductivity, "col", split_axis=0, concat_axis=1, tiled=True
    ).astype(jnp.float32)
    conducts = (conduct_rows, conduct_cols, conductivity.astype(jnp.float32))
    zone_ids = (
        lax.dynamic_slice(
            zone_map, (0, col_index * slab_y + row_index * part_y), (total_x, part_y)
        ),
        lax.dynamic_slice(
            zone_map, (row_index * slab_x + col_index * part_x, 0), (part_x, total_y)
        ),
        lax.dynamic_slice(zone_map, (row_index * slab_x, col_index * slab_y), (slab_x, slab_y)),
    )
    matrices = (line_x, line_y, line_z)
    section_total = 3 * STEPS
    stored = []
    heads = head_start
    for section_index in range(section_total):
        direction = section_index % 3
        stored.append(heads)
        line_field = to_lines(heads, direction)
        if section_index + 1 < section_total:
            widened = line_field.astype(jnp.float32)
            source = (
                widened + time_step * flux_divergence(widened, conducts[direction], direction)
            ).astype(jnp.bfloat16)
            result = line_apply(matrices[direction], source, direction, False).astype(jnp.bfloat16)
            heads = from_lines(result, direction)
    adjoint = cotangent
    zone_accum = jnp.zeros((zone_count,), jnp.float32)
    for section_index in reversed(range(section_total)):
        direction = section_index % 3
        adjoint_lines, state_lines = pair_to_lines(adjoint, stored[section_index], direction)
        backed = line_apply(matrices[direction], adjoint_lines, direction, True)
        column_grad = jnp.sum(
            flux_product(state_lines.astype(jnp.float32), backed, direction), axis=2
        )
        zone_accum = zone_accum + jax.ops.segment_sum(
            column_grad.reshape(-1), zone_ids[direction].reshape(-1), num_segments=zone_count
        )
        updated = (
            backed + time_step * flux_divergence(backed, conducts[direction], direction)
        ).astype(jnp.bfloat16)
        adjoint = from_lines(updated, direction)
    ordered = zone_accum[owner_order]
    zone_grad = lax.psum_scatter(
        ordered, ("row", "col"), scatter_dimension=0, tiled=True
    ) / math.sqrt(total_x * total_y * depth_cells / zone_count)
    return (adjoint, zone_grad)


def solution(mesh):
    placed = (
        P("row", "col", None),
        P("row", "col", None),
        P("row", "col", None),
        P(),
        P(),
        P(),
        P(),
        P(),
    )
    return jax.shard_map(
        on_device,
        mesh=mesh,
        in_specs=placed,
        out_specs=(P("row", "col", None), P(("row", "col"))),
        check_vma=False,
    )
```

profile of v0, /device:TPU:1, one launch (start us, length us, event | category | flops | bytes accessed | tf_op | source)
XLA Modules:
  0.0 554.6 jit_solution(5819712561418701843)
XLA Ops:
  0.7 2.3 copy.167
  3.0 11.9 %all-to-all-start.10 = ((bf16[16,128,128]{2,0,1:T(8,128)(2,1)}), bf16[16,128,128]{2,0,1:T(8,128)(2,1)S(1)}, u32[]{:S(2)}, u32[]{:S(2)}) async-start(bf16[16,128,128]{2,0,1:T(8,128)(2,1)} %copy.167), calls=%async_computation.10 | async-start | bytes 1048576 | tf_op jit(solution)/shard_map/all_to_all | solution.py:58
  16.0 15.1 %all-to-all-done.10 = bf16[16,128,128]{2,0,1:T(8,128)(2,1)S(1)} async-done(((bf16[16,128,128]{2,0,1:T(8,128)(2,1)}), bf16[16,128,128]{2,0,1:T(8,128)(2,1)S(1)}, u32[]{:S(2)}, u32[]{:S(2)}) %all-to-all-start.10) | async-done | bytes 524320 | tf_op jit(solution)/shard_map/all_to_all | solution.py:58
  31.1 5.3 all-to-all-start.4
  36.7 14.8 %all-to-all-done.4 = bf16[16,128,128]{2,0,1:T(8,128)(2,1)} async-done(((bf16[16,128,128]{2,0,1:T(8,128)(2,1)}), bf16[16,128,128]{2,0,1:T(8,128)(2,1)}, u32[]{:S(2)}, u32[]{:S(2)}) %all-to-all-start.4) | async-done | bytes 524320 | tf_op jit(solution)/shard_map/all_to_all | solution.py:96
  51.5 8.2 %all-to-all-start.1 = ((bf16[16,128,128]{2,1,0:T(8,128)(2,1)}), bf16[16,128,128]{2,1,0:T(8,128)(2,1)}, u32[]{:S(2)}, u32[]{:S(2)}) async-start(bf16[16,128,128]{2,1,0:T(8,128)(2,1)} %param.10), calls=%async_computation.1 | async-start | bytes 1048576 | tf_op jit(solution)/shard_map/all_to_all | solution.py:99
  64.5 2.4 convolution_convert_fusion.1
  66.9 2.1 copy.170
  69.3 4.6 all-to-all-start.11
  79.9 10.0 %all-to-all-done.11 = bf16[512,4,128]{2,1,0:T(4,128)(2,1)} async-done(((bf16[512,4,128]{2,1,0:T(4,128)(2,1)}), bf16[512,4,128]{2,1,0:T(4,128)(2,1)}, u32[]{:S(2)}, u32[]{:S(2)}) %all-to-all-start.11) | async-done | bytes 524320 | tf_op jit(solution)/shard_map/all_to_all | solution.py:66
  89.9 6.8 %all-to-all-start = ((bf16[16,128,128]{1,2,0:T(8,128)(2,1)}), bf16[16,128,128]{1,2,0:T(8,128)(2,1)S(1)}, u32[]{:S(2)}, u32[]{:S(2)}) async-start(bf16[16,128,128]{1,2,0:T(8,128)(2,1)} %add_convert_fusion.10), calls=%async_computation | async-start | bytes 1048576 | tf_op jit(solution)/shard_map/all_to_all | solution.py:80
  98.8 7.3 %all-to-all-done = bf16[16,128,128]{1,2,0:T(8,128)(2,1)S(1)} async-done(((bf16[16,128,128]{1,2,0:T(8,128)(2,1)}), bf16[16,128,128]{1,2,0:T(8,128)(2,1)S(1)}, u32[]{:S(2)}, u32[]{:S(2)}) %all-to-all-start) | async-done | bytes 524320 | tf_op jit(solution)/shard_map/all_to_all | solution.py:80
  106.2 4.9 all-to-all-start.12
  115.3 5.4 all-to-all-done.12
  120.7 2.2 convert_bitcast_fusion.2
  122.8 2.5 copy.174
  125.4 2.4 reshape.112
  127.8 3.9 fusion.52
  133.8 2.0 copy.143
  135.8 13.6 %all_to_all.263 = bf16[2,1024,128]{2,0,1:T(2,128)(2,1)S(1)} all-to-all(bf16[2,1024,128]{2,0,1:T(2,128)(2,1)} %copy.143), channel_id=1, replica_groups=mesh['row'=32,'col'=8] {'col'}, dimensions={1} | all-to-all | bytes 1048576 | tf_op jit(solution)/shard_map/all_to_all | solution.py:68
  150.7 4.6 all-to-all-start.3
  155.3 3.5 fusion.23
  160.8 9.8 %all-to-all-done.3 = bf16[16,128,128]{2,0,1:T(8,128)(2,1)} async-done(((bf16[16,128,128]{2,0,1:T(8,128)(2,1)}), bf16[16,128,128]{2,0,1:T(8,128)(2,1)}, u32[]{:S(2)}, u32[]{:S(2)}) %all-to-all-start.3) | async-done | bytes 524320 | tf_op jit(solution)/shard_map/all_to_all | solution.py:75
  170.6 7.9 %all-to-all-start.13 = ((bf16[2,1024,128]{2,0,1:T(2,128)(2,1)}), bf16[2,1024,128]{2,0,1:T(2,128)(2,1)}, u32[]{:S(2)}, u32[]{:S(2)}) async-start(bf16[2,1024,128]{2,0,1:T(2,128)(2,1)} %copy.175), calls=%async_computation.13 | async-start | bytes 1048576 | tf_op jit(solution)/shard_map/all_to_all | solution.py:68
  183.8 2.5 copy.150
  186.3 2.6 copy.151
  192.2 4.6 all-to-all-start.5
  196.8 2.2 copy.176
  199.0 14.5 %all-to-all-done.5 = bf16[512,4,128]{2,1,0:T(4,128)(2,1)} async-done(((bf16[512,4,128]{2,1,0:T(4,128)(2,1)}), bf16[512,4,128]{2,1,0:T(4,128)(2,1)}, u32[]{:S(2)}, u32[]{:S(2)}) %all-to-all-start.5) | async-done | bytes 524320 | tf_op jit(solution)/shard_map/all_to_all | solution.py:66
  217.7 15.6 %all_to_all.264 = bf16[16,128,128]{1,2,0:T(8,128)(2,1)S(1)} all-to-all(bf16[16,128,128]{1,2,0:T(8,128)(2,1)S(1)} %add_convert_fusion.7), channel_id=1, replica_groups=mesh['row'=32,'col'=8] {'col'}, dimensions={0} | all-to-all | bytes 1048576 | tf_op jit(solution)/shard_map/all_to_all | solution.py:80
  239.7 5.0 all-to-all-start.7
  244.7 2.4 convolution_convert_fusion.2
  248.2 6.1 %all-to-all-done.7 = bf16[2,1024,128]{2,0,1:T(2,128)(2,1)} async-done(((bf16[2,1024,128]{2,0,1:T(2,128)(2,1)}), bf16[2,1024,128]{2,0,1:T(2,128)(2,1)}, u32[]{:S(2)}, u32[]{:S(2)}) %all-to-all-start.7) | async-done | bytes 524320 | tf_op jit(solution)/shard_map/all_to_all | solution.py:68
  254.3 4.6 all-to-all-start.14
  261.2 13.3 %all-to-all-done.14 = bf16[16,128,128]{2,0,1:T(8,128)(2,1)} async-done(((bf16[16,128,128]{2,0,1:T(8,128)(2,1)}), bf16[16,128,128]{2,0,1:T(8,128)(2,1)}, u32[]{:S(2)}, u32[]{:S(2)}) %all-to-all-start.14) | async-done | bytes 524320 | tf_op jit(solution)/shard_map/all_to_all | solution.py:58
  274.6 5.8 %all-to-all-start.8 = ((bf16[16,128,128]{2,0,1:T(8,128)(2,1)}), bf16[16,128,128]{2,0,1:T(8,128)(2,1)}, u32[]{:S(2)}, u32[]{:S(2)}) async-start(bf16[16,128,128]{2,0,1:T(8,128)(2,1)} %copy.160), calls=%async_computation.8 | async-start | bytes 1048576 | tf_op jit(solution)/shard_map/all_to_all | solution.py:75
  282.7 12.7 %all-to-all-done.8 = bf16[16,128,128]{2,0,1:T(8,128)(2,1)} async-done(((bf16[16,128,128]{2,0,1:T(8,128)(2,1)}), bf16[16,128,128]{2,0,1:T(8,128)(2,1)}, u32[]{:S(2)}, u32[]{:S(2)}) %all-to-all-start.8) | async-done | bytes 524320 | tf_op jit(solution)/shard_map/all_to_all | solution.py:75
  300.6 2.5 copy.162
  303.2 5.0 fusion.50
  309.2 2.1 copy.180
  311.3 2.5 convolution_convert_fusion
  313.7 2.1 copy.181
  315.9 21.3 %all_to_all.265 = bf16[512,4,128]{2,1,0:T(4,128)(2,1)S(1)} all-to-all(bf16[512,4,128]{2,1,0:T(4,128)(2,1)} %copy.181), channel_id=1, replica_groups=mesh['row'=32,'col'=8] {'row'}, dimensions={0} | all-to-all | bytes 1048576 | tf_op jit(solution)/shard_map/all_to_all | solution.py:66
  338.2 8.1 %all-to-all-start.16 = ((bf16[16,128,128]{2,1,0:T(8,128)(2,1)}), bf16[16,128,128]{2,1,0:T(8,128)(2,1)}, u32[]{:S(2)}, u32[]{:S(2)}) async-start(bf16[16,128,128]{2,1,0:T(8,128)(2,1)} %copy.184), calls=%async_computation.16 | async-start | bytes 1048576 | tf_op jit(solution)/shard_map/all_to_all | solution.py:60
  347.6 2.5 copy.163
  350.2 2.1 add_convert_fusion.5
  353.4 2.5 all-to-all-done.16
  355.9 4.6 all-to-all-start.9
  361.3 2.1 convert_bitcast_fusion
  363.4 2.6 copy.185
  366.0 2.4 reshape.115
  368.4 3.5 fusion.44
  373.6 2.1 copy.186
  376.5 6.6 %all-to-all-start.17 = ((bf16[2,1024,128]{2,0,1:T(2,128)(2,1)}), bf16[2,1024,128]{2,0,1:T(2,128)(2,1)}, u32[]{:S(2)}, u32[]{:S(2)}) async-start(bf16[2,1024,128]{2,0,1:T(2,128)(2,1)} %copy.186), calls=%async_computation.17 | async-start | bytes 1048576 | tf_op jit(solution)/shard_map/all_to_all | solution.py:68
  384.0 11.3 %scatter_custom_fusion.3 = f32[2048]{0:T(1024)S(1)} fusion(s32[2048]{0:T(1024)S(1)} %dynamic-slice_bitcast_fusion.1, f32[2048]{0:T(1024)S(1)} %bitcast.222, f32[]{:T(128)} %constant.17.clone.1), kind=kCustom, calls=%fused_computation.106 | custom fusion | flops 2048 | bytes 8196 | tf_op jit(solution)/shard_map/scatter-add | solution.py:136
  397.4 2.9 multiply_reduce_fusion
  401.0 11.4 %scatter_custom_fusion.5 = f32[2048]{0:T(1024)S(1)} fusion(s32[2048]{0:T(1024)S(1)} %reshape.151, f32[2048]{0:T(1024)S(1)} %reshape.177, f32[]{:T(128)} %constant.17.clone.1), kind=kCustom, calls=%fused_computation.104 | custom fusion | flops 2048 | bytes 8196 | tf_op jit(solution)/shard_map/scatter-add | solution.py:136
  416.4 11.3 %scatter_custom_fusion.1 = f32[2048]{0:T(1024)S(1)} fusion(s32[2048]{0:T(1024)S(1)} %bitcast.216, f32[2048]{0:T(1024)S(1)} %bitcast.223, f32[]{:T(128)} %constant.17.clone.1), kind=kCustom, calls=%fused_computation.108 | custom fusion | flops 2048 | bytes 8196 | tf_op jit(solution)/shard_map/scatter-add | solution.py:136
  427.8 2.2 copy.187
  432.0 11.3 %scatter_custom_fusion = f32[2048]{0:T(1024)S(1)} fusion(s32[2048]{0:T(1024)S(1)} %dynamic-slice_bitcast_fusion.1, f32[2048]{0:T(1024)S(1)} %bitcast.221, f32[]{:T(128)} %constant.17.clone.1), kind=kCustom, calls=%fused_computation.110 | custom fusion | flops 2048 | bytes 8196 | tf_op jit(solution)/shard_map/scatter-add | solution.py:136
  443.3 11.9 %scatter_fusion = f32[2048]{0:T(1024)S(1)} fusion(f32[2048]{0:T(1024)S(1)} %add.207, s32[2048]{0:T(1024)S(1)} %reshape.151, f32[2048]{0:T(1024)S(1)} %reshape.153), kind=kCustom, calls=%fused_computation.3 | custom fusion | flops 2048 | bytes 32768 | tf_op jit(solution)/shard_map/scatter-add | solution.py:136
  455.3 11.6 %scatter_fusion.1 = f32[2048]{0:T(1024)S(1)} fusion(f32[2048]{0:T(1024)S(1)} %add.212, s32[2048]{0:T(1024)S(1)} %bitcast.217, f32[2048]{0:T(1024)S(1)} %bitcast.218), kind=kCustom, calls=%fused_computation.5 | custom fusion | flops 2048 | bytes 32768 | tf_op jit(solution)/shard_map/scatter-add | solution.py:136
  466.9 11.8 %gather_fusion = f32[2048]{0:T(1024)S(1)} fusion(f32[2048]{0:T(1024)S(1)} %add.215, s32[2048]{0:T(1024)S(1)} %fusion.62), kind=kCustom, calls=%fused_computation | custom fusion | bytes 24576 | tf_op jit(solution)/shard_map/gather | solution.py:143
  478.7 75.1 %all-reduce.34 = f32[2048]{0:T(1024)S(1)} all-reduce(f32[2048]{0:T(1024)S(1)} %gather_fusion), channel_id=2, replica_groups=mesh['row'=32,'col'=8] {'row','col'}, use_global_device_ids=true, to_apply=%region_12.13.clone | all-reduce | flops 2048 | bytes 16384
  (125 shorter events, 71.9 us)
Async XLA Ops:
  0.6 112.9 %copy-start = (bf16[1024,1024]{1,0:T(8,128)(2,1)S(1)}, bf16[1024,1024]{1,0:T(8,128)(2,1)}, u32[]{:S(2)}) copy-start(bf16[1024,1024]{1,0:T(8,128)(2,1)} %param.12) | copy-start | bytes 6291460
  0.6 14.2 %copy-start.14 = (bf16[16,128,128]{2,1,0:T(8,128)(2,1)S(1)}, bf16[16,128,128]{2,1,0:T(8,128)(2,1)}, u32[]{:S(2)}) copy-start(bf16[16,128,128]{2,1,0:T(8,128)(2,1)} %param.10) | copy-start | bytes 1572868
  3.0 28.1 %all-to-all-start.10 = ((bf16[16,128,128]{2,0,1:T(8,128)(2,1)}), bf16[16,128,128]{2,0,1:T(8,128)(2,1)S(1)}, u32[]{:S(2)}, u32[]{:S(2)}) async-start(bf16[16,128,128]{2,0,1:T(8,128)(2,1)} %copy.167), calls=%async_computation.10 | async-start | bytes 1048576 | tf_op jit(solution)/shard_map/all_to_all | solution.py:58
  31.1 20.4 %all-to-all-start.4 = ((bf16[16,128,128]{2,0,1:T(8,128)(2,1)}), bf16[16,128,128]{2,0,1:T(8,128)(2,1)}, u32[]{:S(2)}, u32[]{:S(2)}) async-start(bf16[16,128,128]{2,0,1:T(8,128)(2,1)} %copy.148), calls=%async_computation.4 | async-start | bytes 1048576 | tf_op jit(solution)/shard_map/all_to_all | solution.py:96
  36.7 25.6 %copy-start.4 = (f32[32,16,4,128]{3,1,0,2:T(8,128)}, f32[32,16,4,128]{3,1,0,2:T(8,128)S(1)}, u32[]{:S(2)}) copy-start(f32[32,16,4,128]{3,1,0,2:T(8,128)S(1)} %copy.168) | copy-start | bytes 3145732
  51.5 17.8 %all-to-all-start.1 = ((bf16[16,128,128]{2,1,0:T(8,128)(2,1)}), bf16[16,128,128]{2,1,0:T(8,128)(2,1)}, u32[]{:S(2)}, u32[]{:S(2)}) async-start(bf16[16,128,128]{2,1,0:T(8,128)(2,1)} %param.10), calls=%async_computation.1 | async-start | bytes 1048576 | tf_op jit(solution)/shard_map/all_to_all | solution.py:99
  64.5 9.4 %copy-start.15 = (bf16[16,128,128]{2,1,0:T(8,128)(2,1)S(1)}, bf16[16,128,128]{2,1,0:T(8,128)(2,1)}, u32[]{:S(2)}) copy-start(bf16[16,128,128]{2,1,0:T(8,128)(2,1)} %param.10) | copy-start | bytes 1572868
  66.9 9.2 %copy-start.19 = (bf16[128,128]{1,0:T(8,128)(2,1)S(1)}, bf16[128,128]{1,0:T(8,128)(2,1)}, u32[]{:S(2)}) copy-start(bf16[128,128]{1,0:T(8,128)(2,1)} %param.13) | copy-start | bytes 98308
  69.3 20.6 %all-to-all-start.11 = ((bf16[512,4,128]{2,1,0:T(4,128)(2,1)}), bf16[512,4,128]{2,1,0:T(4,128)(2,1)}, u32[]{:S(2)}, u32[]{:S(2)}) async-start(bf16[512,4,128]{2,1,0:T(4,128)(2,1)} %copy.170), calls=%async_computation.11 | async-start | bytes 1048576 | tf_op jit(solution)/shard_map/all_to_all | solution.py:66
  76.1 2.1 copy-start.5
  77.9 1.0 copy-start.2
  89.9 16.3 %all-to-all-start = ((bf16[16,128,128]{1,2,0:T(8,128)(2,1)}), bf16[16,128,128]{1,2,0:T(8,128)(2,1)S(1)}, u32[]{:S(2)}, u32[]{:S(2)}) async-start(bf16[16,128,128]{1,2,0:T(8,128)(2,1)} %add_convert_fusion.10), calls=%async_computation | async-start | bytes 1048576 | tf_op jit(solution)/shard_map/all_to_all | solution.py:80
  106.2 4.9 copy-start.18
  106.2 14.5 %all-to-all-start.12 = ((bf16[16,128,128]{2,1,0:T(8,128)(2,1)}), bf16[16,128,128]{2,1,0:T(8,128)(2,1)}, u32[]{:S(2)}, u32[]{:S(2)}) async-start(bf16[16,128,128]{2,1,0:T(8,128)(2,1)} %copy.173), calls=%async_computation.12 | async-start | bytes 1048576 | tf_op jit(solution)/shard_map/all_to_all | solution.py:60
  131.6 1.0 copy-start.8
  150.7 20.0 %all-to-all-start.3 = ((bf16[16,128,128]{2,0,1:T(8,128)(2,1)}), bf16[16,128,128]{2,0,1:T(8,128)(2,1)}, u32[]{:S(2)}, u32[]{:S(2)}) async-start(bf16[16,128,128]{2,0,1:T(8,128)(2,1)} %copy.146), calls=%async_computation.3 | async-start | bytes 1048576 | tf_op jit(solution)/shard_map/all_to_all | solution.py:75
  170.6 21.6 %all-to-all-start.13 = ((bf16[2,1024,128]{2,0,1:T(2,128)(2,1)}), bf16[2,1024,128]{2,0,1:T(2,128)(2,1)}, u32[]{:S(2)}, u32[]{:S(2)}) async-start(bf16[2,1024,128]{2,0,1:T(2,128)(2,1)} %copy.175), calls=%async_computation.13 | async-start | bytes 1048576 | tf_op jit(solution)/shard_map/all_to_all | solution.py:68
  181.3 1.0 copy-start.11
  188.9 1.9 copy-start.17
  192.2 21.3 %all-to-all-start.5 = ((bf16[512,4,128]{2,1,0:T(4,128)(2,1)}), bf16[512,4,128]{2,1,0:T(4,128)(2,1)}, u32[]{:S(2)}, u32[]{:S(2)}) async-start(bf16[512,4,128]{2,1,0:T(4,128)(2,1)} %copy.152), calls=%async_computation.5 | async-start | bytes 1048576 | tf_op jit(solution)/shard_map/all_to_all | solution.py:66
  213.5 2.0 copy-start.6
  213.5 2.0 copy-start.13
  233.3 1.2 copy-start.1
  233.3 1.5 copy-start.9
  239.7 14.7 %all-to-all-start.7 = ((bf16[2,1024,128]{2,0,1:T(2,128)(2,1)}), bf16[2,1024,128]{2,0,1:T(2,128)(2,1)}, u32[]{:S(2)}, u32[]{:S(2)}) async-start(bf16[2,1024,128]{2,0,1:T(2,128)(2,1)} %copy.157), calls=%async_computation.7 | async-start | bytes 1048576 | tf_op jit(solution)/shard_map/all_to_all | solution.py:68
  254.3 20.3 %all-to-all-start.14 = ((bf16[16,128,128]{2,0,1:T(8,128)(2,1)}), bf16[16,128,128]{2,0,1:T(8,128)(2,1)}, u32[]{:S(2)}, u32[]{:S(2)}) async-start(bf16[16,128,128]{2,0,1:T(8,128)(2,1)} %copy.178), calls=%async_computation.14 | async-start | bytes 1048576 | tf_op jit(solution)/shard_map/all_to_all | solution.py:58
  274.6 20.8 %all-to-all-start.8 = ((bf16[16,128,128]{2,0,1:T(8,128)(2,1)}), bf16[16,128,128]{2,0,1:T(8,128)(2,1)}, u32[]{:S(2)}, u32[]{:S(2)}) async-start(bf16[16,128,128]{2,0,1:T(8,128)(2,1)} %copy.160), calls=%async_computation.8 | async-start | bytes 1048576 | tf_op jit(solution)/shard_map/all_to_all | solution.py:75
  298.2 1.1 copy-start.10
  303.2 5.0 copy-start.12
  338.2 17.7 %all-to-all-start.16 = ((bf16[16,128,128]{2,1,0:T(8,128)(2,1)}), bf16[16,128,128]{2,1,0:T(8,128)(2,1)}, u32[]{:S(2)}, u32[]{:S(2)}) async-start(bf16[16,128,128]{2,1,0:T(8,128)(2,1)} %copy.184), calls=%async_computation.16 | async-start | bytes 1048576 | tf_op jit(solution)/shard_map/all_to_all | solution.py:60
  355.9 20.6 %all-to-all-start.9 = ((bf16[512,4,128]{2,1,0:T(4,128)(2,1)}), bf16[512,4,128]{2,1,0:T(4,128)(2,1)}, u32[]{:S(2)}, u32[]{:S(2)}) async-start(bf16[512,4,128]{2,1,0:T(4,128)(2,1)} %copy.164), calls=%async_computation.9 | async-start | bytes 1048576 | tf_op jit(solution)/shard_map/all_to_all | solution.py:66
  368.4 3.5 copy-start.7
  373.6 10.2 %copy-start.20 = (s32[2048]{0:T(1024)S(1)}, s32[2048]{0:T(1024)}, u32[]{:S(2)}) copy-start(s32[2048]{0:T(1024)} %param.15) | copy-start | bytes 24580
  373.6 10.2 %copy-start.16 = (f32[16,128,127]{1,2,0:T(8,128)S(1)}, f32[16,128,127]{1,2,0:T(8,128)}, u32[]{:S(2)}) copy-start(f32[16,128,127]{1,2,0:T(8,128)} %get-tuple-element.18) | copy-start | bytes 3121156
  376.5 51.3 %all-to-all-start.17 = ((bf16[2,1024,128]{2,0,1:T(2,128)(2,1)}), bf16[2,1024,128]{2,0,1:T(2,128)(2,1)}, u32[]{:S(2)}, u32[]{:S(2)}) async-start(bf16[2,1024,128]{2,0,1:T(2,128)(2,1)} %copy.186), calls=%async_computation.17 | async-start | bytes 1048576 | tf_op jit(solution)/shard_map/all_to_all | solution.py:68
  413.5 16.4 %copy-start.3 = (f32[16,128,128]{1,2,0:T(8,128)S(1)}, f32[16,128,128]{1,2,0:T(8,128)}, u32[]{:S(2)}) copy-start(f32[16,128,128]{1,2,0:T(8,128)} %copy-done.2) | copy-start | bytes 3145732
where the time goes:
time: 566 us; the launch traced here: 555 us
  blocking collectives  126 us (22%)
  other arithmetic  117 us (21%)
  waiting for transfers between devices  113 us (20%)
  starting transfers between devices  93.7 us (17%)
  local copies, waits for them, and re-layouts  84.6 us (15%)
  matrix products  20 us (4%)
    unnamed x1, blocking collectives  75.1 us
    scatter-add x6, other arithmetic, on_device(): jax.ops.segment_sum(column_grad.reshape(-1), zone_ids[direction].reshape(...  68.8 us
    all_to_all x2, waiting for transfers between devices, to_lines(): return lax.all_to_all(heads, 'row', split_axis=1, concat_axis=0, tiled=True)  28.4 us
    all_to_all x3, waiting for transfers between devices, from_lines(): return lax.all_to_all(heads, 'row', split_axis=0, concat_axis=1, tiled=True)  25.2 us
    all_to_all x2, waiting for transfers between devices, pair_to_lines(): lax.all_to_all(adjoint, 'row', split_axis=1, concat_axis=0, tiled=True)  22.5 us
    all_to_all x1, blocking collectives, from_lines(): return lax.all_to_all(heads, 'row', split_axis=0, concat_axis=1, tiled=True)  21.3 us
    all_to_all x3, starting transfers between devices, from_lines(): return lax.all_to_all(heads, 'col', split_axis=1, concat_axis=0, tiled=True)  19.6 us
    all_to_all x2, starting transfers between devices, to_lines(): return lax.all_to_all(heads, 'row', split_axis=1, concat_axis=0, tiled=True)  16.5 us
  transfers between devices with their start and end apart: 15, of which 13 were waited for; matrix products, arithmetic and copies ran while one was open for 21% of the time, Pallas kernels for 0%

commit v1 on v0

v1 whole, which is shorter than its diff:
```python
import functools
import math

import jax
import jax.numpy as jnp
from jax import lax
from jax.experimental import pallas as pl
from jax.experimental.pallas import tpu as pltpu
from jax.sharding import PartitionSpec as P

MESH = pl.DeviceIdType.MESH
BF = jnp.bfloat16
F32 = jnp.float32
HALF_STEP = 0.075
PAD = 8


def dot_nn(a, b):
    return lax.dot_general(a, b, (((1,), (0,)), ((), ())), preferred_element_type=F32)


def dot_nt(a, b):
    return lax.dot_general(a, b, (((1,), (1,)), ((), ())), preferred_element_type=F32)


def dot_tn(a, b):
    return lax.dot_general(a, b, (((0,), (0,)), ((), ())), preferred_element_type=F32)


def loop(count, body, unroll=1):
    def step(i, carry):
        body(i)
        return carry

    lax.fori_loop(0, count, step, 0, unroll=unroll)


def split_two(values):
    high = values.astype(BF)
    low = (values - high.astype(F32)).astype(BF)
    return high, low


def kernel(
    rows, cols, scale,
    head_hbm, cot_hbm, cond_hbm, lx_hbm, ly_hbm, lz_hbm, zmap_hbm, owner_hbm,
    out_ref, zout_ref,
    head, cond, state3, back3, back0, cot, lx, ly, lz, zone_s, zone_y, zone_lines, owner,
    rs, rr, cs, cr, turn, cfx, cfz_s, cfy, cfz_y,
    field1, field4, grad4, grad1, back5, src_y,
    q_y, v_s, v_y, lo_s, lo_y, lo_own, zacc, z_send, z_mid, z_row, z_col,
    local_sem, rs_sem, rr_sem, cs_sem, cr_sem, hs_sem, hr_sem, zs_sem, zr_sem,
):
    row = lax.axis_index("row")
    col = lax.axis_index("col")
    slab_x, slab_y, depth = head_hbm.shape
    part_y = slab_y // rows
    part_x = slab_x // cols
    total_x = lx.shape[0]
    total_y = ly.shape[0]

    def row_peer(i):
        return lax.rem(row + i, rows)

    def col_peer(i):
        return lax.rem(col + i, cols)

    loads = {}

    def load(slot, src, dst):
        copy = pltpu.make_async_copy(src, dst, local_sem.at[slot])
        copy.start()
        loads[slot] = copy

    inner = pl.ds(1, slab_x)
    load(0, head_hbm, head.at[inner])
    load(1, cond_hbm, cond.at[inner])
    load(2, cot_hbm, cot)
    load(3, lz_hbm, lz)
    load(4, lx_hbm, lx)
    load(5, ly_hbm, ly)
    load(6, zmap_hbm.at[pl.ds(row * slab_x, slab_x), pl.ds(col * slab_y, slab_y)], zone_s)
    load(7, zmap_hbm.at[pl.ds(row * slab_x + (col * part_x // 8) * 8, 8)], zone_y)
    load(8, owner_hbm, owner)

    barrier = pltpu.get_barrier_semaphore()

    def greet_row(i):
        pl.semaphore_signal(barrier, inc=1, device_id=(row_peer(i + 1), col), device_id_type=MESH)

    def greet_col(i):
        pl.semaphore_signal(barrier, inc=1, device_id=(row, col_peer(i + 1)), device_id_type=MESH)

    loop(rows - 1, greet_row)
    loop(cols - 1, greet_col)
    pl.semaphore_wait(barrier, rows + cols - 2)

    def send_row(k):
        def one(i):
            r = row_peer(i + 1)
            pltpu.make_async_remote_copy(
                src_ref=rs.at[k, r], dst_ref=rr.at[k, row],
                send_sem=rs_sem.at[k], recv_sem=rr_sem.at[k],
                device_id=(r, col), device_id_type=MESH,
            ).start()

        loop(rows - 1, one)
        rr[k, row] = rs[k, row]

    def row_wait(k):
        part = pl.ds(0, rows - 1)
        return pltpu.make_async_remote_copy(
            src_ref=rs.at[k, part], dst_ref=rr.at[k, part],
            send_sem=rs_sem.at[k], recv_sem=rr_sem.at[k],
            device_id=(row, col), device_id_type=MESH,
        )

    def send_col(j, src, offset):
        def one(i):
            c = col_peer(i + 1)
            pltpu.make_async_remote_copy(
                src_ref=src.at[pl.ds(offset + c * part_x, part_x)],
                dst_ref=cr.at[j, pl.ds(col * part_x, part_x)],
                send_sem=cs_sem.at[j], recv_sem=cr_sem.at[j],
                device_id=(row, c), device_id_type=MESH,
            ).start()

        loop(cols - 1, one)
        cr[j, pl.ds(col * part_x, part_x)] = src[pl.ds(offset + col * part_x, part_x)]

    def col_wait(j):
        part = pl.ds(0, (cols - 1) * part_x)
        return pltpu.make_async_remote_copy(
            src_ref=cr.at[j, part], dst_ref=cr.at[j, part],
            send_sem=cs_sem.at[j], recv_sem=cr_sem.at[j],
            device_id=(row, col), device_id_type=MESH,
        )

    def halo_copies(h, buf):
        up = lax.rem(row + 1, rows)
        down = lax.rem(row + rows - 1, rows)
        return (
            pltpu.make_async_remote_copy(
                src_ref=buf.at[slab_x], dst_ref=buf.at[0],
                send_sem=hs_sem.at[h, 0], recv_sem=hr_sem.at[h, 0],
                device_id=(up, col), device_id_type=MESH,
            ),
            pltpu.make_async_remote_copy(
                src_ref=buf.at[1], dst_ref=buf.at[slab_x + 1],
                send_sem=hs_sem.at[h, 1], recv_sem=hr_sem.at[h, 1],
                device_id=(down, col), device_id_type=MESH,
            ),
        )

    def send_halo(h, buf):
        for copy in halo_copies(h, buf):
            copy.start()

    def wait_halo(h, buf):
        for copy in halo_copies(h, buf):
            copy.wait_recv()

    def next_lane(f):
        return pltpu.roll(f, f.shape[1] - 1, axis=1)

    def prev_lane(f):
        return pltpu.roll(f, 1, axis=1)

    def apply_z(f, faces):
        flux = faces * (next_lane(f) - f)
        return f + flux - prev_lane(flux)

    def lane_mask(shape):
        lane = lax.broadcasted_iota(jnp.int32, shape, 1)
        return jnp.where(lane < depth - 1, 1.0, 0.0).astype(F32)

    def plane_x(buf, x):
        below = buf[x].astype(F32)
        mid = buf[x + 1].astype(F32)
        above = buf[x + 2].astype(F32)
        return mid + cfx[x + 1] * (above - mid) - cfx[x] * (mid - below)

    ones8 = jnp.ones((8, depth), BF)

    def depth_sum(products):
        high, low = split_two(products)
        return dot_nt(ones8, high) + dot_nt(ones8, low)

    def turn_in(x, plane):
        turn[pl.ds(x, slab_y, stride=slab_x), :] = plane

    def turn_out(x):
        return turn[pl.ds(x, slab_y, stride=slab_x), :]

    block = part_y * slab_x

    def turned_to_send(k):
        def one(r):
            piece = turn[pl.ds(pl.multiple_of(r * block, block), block), :]
            rs[k, r] = piece.astype(BF).reshape(part_y, slab_x, depth)

        loop(rows, one, 4)

    def received_to_turn(k):
        def one(r):
            piece = rr[k, r].reshape(block, depth).astype(F32)
            turn[pl.ds(pl.multiple_of(r * block, block), block), :] = piece

        loop(rows, one, 4)

    x_chunk = 128
    peers_chunk = x_chunk // slab_x

    def line_x_step(k_in, k_out, transpose):
        rhs = jnp.concatenate(
            [rr[k_in, :, y].reshape(total_x, depth) for y in range(part_y)], axis=1
        )

        def one(m):
            part = pl.ds(pl.multiple_of(m * x_chunk, x_chunk), x_chunk)
            if transpose:
                res = dot_tn(lx[:, part], rhs)
            else:
                res = dot_nn(lx[part, :], rhs)
            res = res.astype(BF)
            for y in range(part_y):
                piece = res[:, y * depth:(y + 1) * depth].reshape(peers_chunk, slab_x, depth)
                rs[k_out, pl.ds(m * peers_chunk, peers_chunk), y] = piece

        loop(total_x // x_chunk, one)

    y_chunk = 256

    def line_y_chunk(m, transpose):
        part = pl.ds(pl.multiple_of(m * y_chunk, y_chunk), y_chunk)
        if transpose:
            return dot_tn(ly[:, part], src_y[...])
        return dot_nn(ly[part, :], src_y[...])

    def line_y_to_field(field, transpose):
        def one(m):
            res = line_y_chunk(m, transpose)
            for x in range(part_x):
                field[x, pl.ds(pl.multiple_of(PAD + m * y_chunk, 8), y_chunk), :] = res[
                    :, x * depth:(x + 1) * depth
                ]

        loop(total_y // y_chunk, one)
        pad_field(field)

    def pad_field(field):
        for x in range(part_x):
            field[x, 0:PAD, :] = jnp.zeros((PAD, depth), F32)
            field[x, PAD + total_y:, :] = jnp.broadcast_to(
                field[x, PAD + total_y - 1:PAD + total_y, :], (PAD, depth)
            )

    def received_to_field(j, field):
        def one(c):
            for x in range(part_x):
                field[x, pl.ds(pl.multiple_of(PAD + c * slab_y, 8), slab_y), :] = cr[
                    j, c * part_x + x
                ].astype(F32)

        loop(cols, one, 2)
        pad_field(field)

    def apply_y(field, x, c):
        base = pl.multiple_of(PAD + c * slab_y, 8)
        mid = field[x, pl.ds(base, slab_y), :]
        above = field[x, pl.ds(base + 1, slab_y), :]
        below = field[x, pl.ds(base - 1, slab_y), :]
        face = cfy[x, pl.ds(base, slab_y), :]
        face_below = cfy[x, pl.ds(base - 1, slab_y), :]
        return mid + face * (above - mid) - face_below * (mid - below)

    def grad_y(field, grad, x, c):
        base = pl.multiple_of(PAD + c * slab_y, 8)
        first = field[x, pl.ds(base + 1, slab_y), :] - field[x, pl.ds(base, slab_y), :]
        second = grad[x, pl.ds(base + 1, slab_y), :] - grad[x, pl.ds(base, slab_y), :]
        return depth_sum(first * second)

    def set_src_y(x, c, values):
        src_y[pl.ds(pl.multiple_of(c * slab_y, slab_y), slab_y), x * depth:(x + 1) * depth] = (
            values.astype(BF)
        )

    def low_codes(zones):
        code = jnp.broadcast_to(zones & (depth - 1), (depth, depth))
        return jnp.where(
            code == lax.broadcasted_iota(jnp.int32, (depth, depth), 0), 1.0, 0.0
        ).astype(BF)

    def high_codes(zones):
        code = jnp.broadcast_to(zones // depth, (16, depth))
        return jnp.where(code == lax.broadcasted_iota(jnp.int32, (16, depth), 0), 1.0, 0.0)

    def zone_add(values, zones, codes):
        spread = jnp.concatenate([values, values], axis=0) * high_codes(zones)
        high, low = split_two(spread)
        zacc[...] += dot_nt(jnp.concatenate([high, low], axis=0), codes)

    def zone_s_row(x):
        return zone_s[pl.ds(x, 1), :]

    def zone_y_row(x, c):
        return zone_lines[pl.ds(c * part_x + x, 1), :]

    def pick_zone_lines():
        groups = 8 // part_x
        for x in range(part_x):
            line = jnp.zeros((1, total_y), jnp.int32)
            for g in range(groups):
                mine = jnp.where(lax.rem(col, groups) == g, 1, 0)
                line = line + mine * zone_y[g * part_x + x:g * part_x + x + 1, :]
            for c in range(cols):
                zone_lines[c * part_x + x:c * part_x + x + 1, :] = line[
                    :, c * slab_y:(c + 1) * slab_y
                ]

    loads[0].wait()
    loads[1].wait()
    send_halo(0, head)
    send_halo(1, cond)
    loads[2].wait()
    send_col(1, cot, 0)
    send_col(0, cond, 1)
    loads[3].wait()

    def faces_z_slab(x):
        c = cond[1 + x].astype(F32)
        cfz_s[x] = HALF_STEP * (c + next_lane(c)) * lane_mask(c.shape)

    loop(slab_x, faces_z_slab, 2)

    wait_halo(1, cond)

    def faces_x_slab(j):
        at_end = ((j == 0) & (row == 0)) | ((j == slab_x) & (row == rows - 1))
        keep = jnp.where(at_end, 0.0, HALF_STEP).astype(F32)
        cfx[j] = keep * (cond[j].astype(F32) + cond[j + 1].astype(F32))

    loop(slab_x + 1, faces_x_slab)
    wait_halo(0, head)

    def first_source(x):
        turn_in(x, plane_x(head, x))

    loop(slab_x, first_source, 2)
    turned_to_send(0)
    send_row(0)

    zacc[...] = jnp.zeros(zacc.shape, F32)
    col_wait(0).wait_recv()

    def cond_lines(c):
        for x in range(part_x):
            own = cr[0, c * part_x + x].astype(F32)
            cfz_y[c * part_x + x] = HALF_STEP * (own + next_lane(own)) * lane_mask(own.shape)

    loop(cols, cond_lines)
    received_to_field(0, field1)

    def faces_y(c):
        for x in range(part_x):
            base = pl.multiple_of(PAD + c * slab_y, 8)
            cfy[x, pl.ds(base, slab_y), :] = HALF_STEP * (
                field1[x, pl.ds(base, slab_y), :] + field1[x, pl.ds(base + 1, slab_y), :]
            )

    loop(cols, faces_y)
    for x in range(part_x):
        cfy[x, 0:PAD, :] = jnp.zeros((PAD, depth), F32)
        cfy[x, PAD + total_y - 1:PAD + total_y, :] = jnp.zeros((1, depth), F32)
        cfy[x, PAD + total_y:, :] = jnp.zeros((PAD, depth), F32)

    col_wait(1).wait_recv()

    def adjoint5(c):
        for x in range(part_x):
            backed = dot_nn(cr[1, c * part_x + x], lz[...])
            back5[c * part_x + x] = backed
            set_src_y(x, c, apply_z(backed, cfz_y[c * part_x + x]))

    loop(cols, adjoint5)
    loads[5].wait()
    line_y_to_field(grad4, True)

    def adjoint4(c):
        for x in range(part_x):
            cs[0, c * part_x + x] = apply_y(grad4, x, c).astype(BF)

    loop(cols, adjoint4)
    send_col(2, cs.at[0], 0)

    loads[4].wait()
    row_wait(0).wait_recv()
    line_x_step(0, 1, False)
    send_row(1)

    col_wait(2).wait_recv()

    def adjoint4_turn(x):
        turn_in(x, cr[2, x].astype(F32))

    loop(slab_x, adjoint4_turn, 2)
    turned_to_send(2)
    send_row(2)

    loads[6].wait()
    loads[7].wait()
    loads[8].wait()

    def codes_s(x):
        lo_s[x] = low_codes(zone_s_row(x))

    def codes_y(c):
        for x in range(part_x):
            lo_y[c * part_x + x] = low_codes(zone_y_row(x, c))

    def codes_own(g):
        lo_own[g] = low_codes(owner[pl.ds(g, 1), :])

    pick_zone_lines()
    loop(slab_x, codes_s)
    loop(cols, codes_y)
    loop(16, codes_own)

    row_wait(1).wait_recv()
    received_to_turn(1)

    def state1_plane(x):
        cs[1, x] = turn_out(x).astype(BF)

    loop(slab_x, state1_plane, 2)
    send_col(3, cs.at[1], 0)
    col_wait(3).wait_recv()
    received_to_field(3, field1)

    def source1(c):
        for x in range(part_x):
            set_src_y(x, c, apply_y(field1, x, c))

    loop(cols, source1)

    def lines1(m):
        res = line_y_chunk(m, False).astype(BF)
        blocks = y_chunk // slab_y
        for b in range(blocks):
            for x in range(part_x):
                cs[2, (m * blocks + b) * part_x + x] = res[
                    b * slab_y:(b + 1) * slab_y, x * depth:(x + 1) * depth
                ]

    loop(total_y // y_chunk, lines1)
    send_col(4, cs.at[2], 0)

    row_wait(2).wait_recv()
    line_x_step(2, 3, True)
    send_row(3)

    col_wait(4).wait_recv()

    def state3_plane(x):
        source = apply_z(cr[4, x].astype(F32), cfz_s[x]).astype(BF)
        state3[1 + x] = dot_nt(source, lz[...]).astype(BF)

    loop(slab_x, state3_plane, 4)
    send_halo(2, state3)
    wait_halo(2, state3)

    def source3(x):
        turn_in(x, plane_x(state3, x))

    loop(slab_x, source3, 2)
    turned_to_send(4)
    send_row(4)

    row_wait(3).wait_recv()
    received_to_turn(3)

    def back3_plane(x):
        back3[1 + x] = turn_out(x).astype(BF)

    loop(slab_x, back3_plane, 2)
    send_halo(3, back3)
    wait_halo(3, back3)

    def face_sum(state, back, j):
        at_end = ((j == 0) & (row == 0)) | ((j == slab_x) & (row == rows - 1))
        keep = jnp.where(at_end, 0.0, 1.0).astype(F32)
        first = state[j + 1].astype(F32) - state[j].astype(F32)
        second = back[j + 1].astype(F32) - back[j].astype(F32)
        return keep * depth_sum(first * second)

    def faces_to_columns(state, back, keep_old):
        def one(j, before):
            here = face_sum(state, back, j + 1)
            total = here + before
            if keep_old:
                total = total + v_s[j]
            v_s[j] = total
            return here

        lax.fori_loop(0, slab_x, one, face_sum(state, back, 0), unroll=2)

    def adjoint3(x):
        source = plane_x(back3, x).astype(BF)
        backed = dot_nn(source, lz[...])
        state = cr[4, x].astype(F32)
        first = next_lane(state) - state
        second = next_lane(backed) - backed
        v_s[x] = 2.0 * depth_sum(first * second * lane_mask(state.shape))
        cs[3, x] = apply_z(backed, cfz_s[x]).astype(BF)

    loop(slab_x, adjoint3, 2)
    send_col(5, cs.at[3], 0)
    faces_to_columns(state3, back3, True)

    row_wait(4).wait_recv()
    line_x_step(4, 5, False)
    send_row(5)

    col_wait(5).wait_recv()

    def source_adj1(c):
        for x in range(part_x):
            set_src_y(x, c, cr[5, c * part_x + x])

    loop(cols, source_adj1)
    line_y_to_field(grad1, True)

    def adjoint1(c):
        for x in range(part_x):
            cs[4, c * part_x + x] = apply_y(grad1, x, c).astype(BF)

    loop(cols, adjoint1)
    send_col(6, cs.at[4], 0)

    def column_y1(c):
        for x in range(part_x):
            q_y[c * part_x + x] = grad_y(field1, grad1, x, c)

    loop(cols, column_y1)

    col_wait(6).wait_recv()

    def adjoint1_turn(x):
        turn_in(x, cr[6, x].astype(F32))

    loop(slab_x, adjoint1_turn, 2)
    turned_to_send(6)
    send_row(6)

    def zones_s(x):
        zone_add(v_s[x], zone_s_row(x), lo_s[x])

    loop(slab_x, zones_s)

    row_wait(5).wait_recv()
    received_to_turn(5)

    def state4_plane(x):
        cs[5, x] = turn_out(x).astype(BF)

    loop(slab_x, state4_plane, 2)
    send_col(7, cs.at[5], 0)
    col_wait(7).wait_recv()
    received_to_field(7, field4)

    def source4(c):
        for x in range(part_x):
            set_src_y(x, c, apply_y(field4, x, c))

    loop(cols, source4)

    row_wait(6).wait_recv()
    line_x_step(6, 7, True)
    send_row(7)

    def lines4(m):
        res = line_y_chunk(m, False).astype(BF).astype(F32)
        blocks = y_chunk // slab_y
        for b in range(blocks):
            for x in range(part_x):
                index = (m * blocks + b) * part_x + x
                state = res[b * slab_y:(b + 1) * slab_y, x * depth:(x + 1) * depth]
                backed = back5[index]
                first = next_lane(state) - state
                second = next_lane(backed) - backed
                v_y[index] = 2.0 * depth_sum(first * second * lane_mask(state.shape))

    loop(total_y // y_chunk, lines4)

    def column_y4(c):
        for x in range(part_x):
            q_y[c * part_x + x] = q_y[c * part_x + x] + grad_y(field4, grad4, x, c)

    loop(cols, column_y4)
    for x in range(part_x):
        line = jnp.concatenate([q_y[c * part_x + x] for c in range(cols)], axis=1)
        line = line + prev_lane(line)
        for c in range(cols):
            v_y[c * part_x + x] = v_y[c * part_x + x] + line[:, c * slab_y:(c + 1) * slab_y]

    def zones_y(c):
        for x in range(part_x):
            zone_add(v_y[c * part_x + x], zone_y_row(x, c), lo_y[c * part_x + x])

    loop(cols, zones_y)

    row_wait(7).wait_recv()
    received_to_turn(7)

    def back0_plane(x):
        back0[1 + x] = turn_out(x).astype(BF)

    loop(slab_x, back0_plane, 2)
    send_halo(4, back0)
    wait_halo(4, back0)
    faces_to_columns(head, back0, False)
    loop(slab_x, zones_s)

    sums = zacc[0:16, :] + zacc[16:32, :]
    high, low = split_two(sums * (-HALF_STEP * scale))
    parts = jnp.concatenate([high, low], axis=0)

    def to_owner(g):
        spread = dot_nn(parts, lo_own[g])
        spread = (spread[0:16] + spread[16:32]) * high_codes(owner[pl.ds(g, 1), :])
        z_send[g] = jnp.broadcast_to(jnp.sum(spread, axis=0, keepdims=True), (8, depth))

    loop(16, to_owner)

    def send_zone_row(i):
        r = row_peer(i + 1)
        pltpu.make_async_remote_copy(
            src_ref=z_send.at[r // 2], dst_ref=z_row.at[row],
            send_sem=zs_sem.at[0], recv_sem=zr_sem.at[0],
            device_id=(r, col), device_id_type=MESH,
        ).start()

    loop(rows - 1, send_zone_row)
    z_row[row] = z_send[row // 2]

    def last_plane(x):
        out_ref[x] = plane_x(back0, x).astype(BF)

    loop(slab_x, last_plane, 2)

    def zone_wait(phase, ref, count):
        part = pl.ds(0, count)
        return pltpu.make_async_remote_copy(
            src_ref=ref.at[part], dst_ref=ref.at[part],
            send_sem=zs_sem.at[phase], recv_sem=zr_sem.at[phase],
            device_id=(row, col), device_id_type=MESH,
        )

    zone_wait(0, z_row, rows - 1).wait_recv()
    z_mid[...] = jnp.sum(z_row[...], axis=0)

    def send_zone_col(i):
        c = col_peer(i + 1)
        pltpu.make_async_remote_copy(
            src_ref=z_mid, dst_ref=z_col.at[col],
            send_sem=zs_sem.at[1], recv_sem=zr_sem.at[1],
            device_id=(row, c), device_id_type=MESH,
        ).start()

    loop(cols - 1, send_zone_col)
    z_col[col] = z_mid[...]
    zone_wait(1, z_col, cols - 1).wait_recv()
    final = jnp.sum(z_col[...], axis=0)
    offset = lax.rem(row, 2) * (depth // 2) + col * 8
    zout_ref[...] = pltpu.roll(final, lax.rem(depth - offset, depth), axis=1)

    for k in range(8):
        row_wait(k).wait_send()
        col_wait(k).wait_send()
    for h, buf in enumerate((head, cond, state3, back3, back0)):
        for copy in halo_copies(h, buf):
            copy.wait_send()
    zone_wait(0, z_row, rows - 1).wait_send()
    zone_wait(1, z_col, cols - 1).wait_send()


def on_device(
    rows, cols, head_start, cotangent, conductivity, line_x, line_y, line_z, zone_map, owner_order
):
    slab_x, slab_y, depth = head_start.shape
    total_x, total_y = zone_map.shape
    zone_count = owner_order.shape[0]
    part_x = slab_x // cols
    part_y = slab_y // rows
    scale = 1.0 / math.sqrt(total_x * total_y * depth / zone_count)
    groups = zone_count // depth
    padded = pltpu.VMEM((slab_x + 2, slab_y, depth), BF)
    field = pltpu.VMEM((part_x, total_y + 2 * PAD, depth), F32)
    slab32 = pltpu.VMEM((slab_x, slab_y, depth), F32)
    sums = pltpu.VMEM((slab_x, 8, depth), F32)
    codes = pltpu.VMEM((16, depth, depth), BF)
    scratch = [
        padded, padded, padded, padded, padded,
        pltpu.VMEM((slab_x, slab_y, depth), BF),
        pltpu.VMEM(line_x.shape, BF),
        pltpu.VMEM(line_y.shape, BF),
        pltpu.VMEM(line_z.shape, BF),
        pltpu.VMEM((slab_x, slab_y), jnp.int32),
        pltpu.VMEM((8, total_y), jnp.int32),
        pltpu.VMEM((slab_x, slab_y), jnp.int32),
        pltpu.VMEM((groups, depth), jnp.int32),
        pltpu.VMEM((8, rows, part_y, slab_x, depth), BF),
        pltpu.VMEM((8, rows, part_y, slab_x, depth), BF),
        pltpu.VMEM((6, slab_x, slab_y, depth), BF),
        pltpu.VMEM((8, slab_x, slab_y, depth), BF),
        pltpu.VMEM((slab_x * slab_y, depth), F32),
        pltpu.VMEM((slab_x + 1, slab_y, depth), F32),
        slab32,
        field,
        slab32,
        field, field, field, field,
        slab32,
        pltpu.VMEM((total_y, part_x * depth), BF),
        sums, sums, sums,
        codes, codes, codes,
        pltpu.VMEM((32, depth), F32),
        pltpu.VMEM((groups, 8, depth), F32),
        pltpu.VMEM((8, depth), F32),
        pltpu.VMEM((rows, 8, depth), F32),
        pltpu.VMEM((cols, 8, depth), F32),
        pltpu.SemaphoreType.DMA((9,)),
        pltpu.SemaphoreType.DMA((8,)),
        pltpu.SemaphoreType.DMA((8,)),
        pltpu.SemaphoreType.DMA((8,)),
        pltpu.SemaphoreType.DMA((8,)),
        pltpu.SemaphoreType.DMA((5, 2)),
        pltpu.SemaphoreType.DMA((5, 2)),
        pltpu.SemaphoreType.DMA((2,)),
        pltpu.SemaphoreType.DMA((2,)),
    ]
    adjoint, zones = pl.pallas_call(
        functools.partial(kernel, rows, cols, scale),
        out_shape=(
            jax.ShapeDtypeStruct((slab_x, slab_y, depth), BF),
            jax.ShapeDtypeStruct((8, depth), F32),
        ),
        in_specs=[pl.BlockSpec(memory_space=pl.ANY)] * 8,
        out_specs=(
            pl.BlockSpec(memory_space=pltpu.VMEM),
            pl.BlockSpec(memory_space=pltpu.VMEM),
        ),
        scratch_shapes=scratch,
        compiler_params=pltpu.CompilerParams(
            collective_id=0, has_side_effects=True, vmem_limit_bytes=56 << 20
        ),
        name="adjoint_lines",
    )(
        head_start, cotangent, conductivity, line_x, line_y, line_z, zone_map,
        owner_order.reshape(groups, depth),
    )
    return adjoint, zones[0, : zone_count // (rows * cols)]


def solution(mesh):
    slab = P("row", "col", None)
    return jax.shard_map(
        functools.partial(on_device, mesh.shape["row"], mesh.shape["col"]),
        mesh=mesh,
        in_specs=(slab, slab, slab, P(), P(), P(), P(), P()),
        out_specs=(slab, P(("row", "col"))),
        check_vma=False,
    )
```

time: 566 us -> 166 us (0.29); the launches traced: 555 us -> 166 us
  Pallas kernels: 0 us -> 162 us
  blocking collectives: 126 us -> 0 us
  other arithmetic: 117 us -> 0 us
  waiting for transfers between devices: 113 us -> 0 us
  starting transfers between devices: 93.7 us -> 0 us
  local copies, waits for them, and re-layouts: 84.6 us -> 3.07 us
  matrix products: 20 us -> 0 us
    pallas_call x0 -> x1, Pallas kernels: none -> 162 us  [on_device(): pl.pallas_call(functools.partial(kernel, rows, cols, scale), out_shape=(j...]
    all_to_all x15 -> x0, waiting for transfers between devices: 113 us -> none  [the longest x2 28.4 us: to_lines(): return lax.all_to_all(heads, 'row', split_axis=1, concat_axis=0, tiled=True)]
    all_to_all x15 -> x0, starting transfers between devices: 93.7 us -> none  [the longest x3 19.6 us: from_lines(): return lax.all_to_all(heads, 'col', split_axis=1, concat_axis=0, tiled=True)]
    unnamed x1 -> x0, blocking collectives: 75.1 us -> none
    scatter-add x6 -> x0, other arithmetic: 68.8 us -> none  [on_device(): jax.ops.segment_sum(column_grad.reshape(-1), zone_ids[direction].reshape(...]
    all_to_all x3 -> x0, blocking collectives: 50.5 us -> none  [the longest x1 21.3 us: from_lines(): return lax.all_to_all(heads, 'row', split_axis=0, concat_axis=1, tiled=True)]
    convert_element_type x22 -> x0, local copies, waits for them, and re-layouts: 37.3 us -> none  [the longest x7 13.3 us: on_device(): widened = line_field.astype(jnp.float32)]
    mul x10 -> x0, other arithmetic: 21.5 us -> none  [the longest x5 14 us: flux_product(): jnp.diff(states, axis=direction) * jnp.diff(backed, axis=direction)]
  transfers between devices with their start and end apart: 15 -> 0, of which waited for: 13 -> 0; matrix products, arithmetic and copies ran while one was open for 21% -> 0% of each run, Pallas kernels for 0% -> 0%
where the time goes in v1:
time: 166 us
  Pallas kernels  162 us (98%)
  local copies, waits for them, and re-layouts  3.07 us (2%)
    pallas_call x1, Pallas kernels, on_device(): pl.pallas_call(functools.partial(kernel, rows, cols, scale), out_shape=(j...  162 us

profile of v1, /device:TPU:1, one launch (start us, length us, event | category | flops | bytes accessed | tf_op | source)
XLA Modules:
  0.0 166.1 jit_solution(4115031774030321093)
XLA Ops:
  0.6 162.4 %adjoint_lines.1 = (bf16[16,128,128]{2,1,0:T(8,128)(2,1)}, f32[8,128]{1,0:T(8,128)}) custom-call(bf16[16,128,128]{2,1,0:T(8,128)(2,1)} %head_hbm.1, bf16[16,128,128]{2,1,0:T(8,128)(2,1)} %cot_hbm.1, bf16[16,128,128]{2,1,0:T(8,128)(2,1)} %cond_hbm.1, bf16[512,512]{1,0:T(8,128)(2,1)} %lx_hbm.1, bf16[1024,1024]{1,0:T(8,128)(2,1)} %ly_hbm.1, ...), custom_call_target="tpu_custom_call" | custom-call | tf_op jit(solution)/shard_map/adjoint_lines/pallas_call | solution.py:741
  163.0 1.2 slice_bitcast_fusion
  164.2 1.9 %copy.11 = bf16[16,128,128]{2,1,0:T(8,128)(2,1)} copy(bf16[16,128,128]{2,1,0:T(8,128)(2,1)} %get-tuple-element.8) | data formatting | bytes 1048576

commit v2 on v0

v2 whole, which is shorter than its diff:
```python
import functools
import math

import jax
import jax.numpy as jnp
from jax import lax
from jax.experimental import pallas as pl
from jax.experimental.pallas import tpu as pltpu
from jax.sharding import PartitionSpec as P

MESH = pl.DeviceIdType.MESH
BF = jnp.bfloat16
F32 = jnp.float32
HALF_STEP = 0.075
PAD = 8


def dot_nn(a, b):
    return lax.dot_general(a, b, (((1,), (0,)), ((), ())), preferred_element_type=F32)


def dot_nt(a, b):
    return lax.dot_general(a, b, (((1,), (1,)), ((), ())), preferred_element_type=F32)


def dot_tn(a, b):
    return lax.dot_general(a, b, (((0,), (0,)), ((), ())), preferred_element_type=F32)


def loop(count, body, unroll=1):
    def step(i, carry):
        body(i)
        return carry

    lax.fori_loop(0, count, step, 0, unroll=unroll)


def split_two(values):
    high = values.astype(BF)
    low = (values - high.astype(F32)).astype(BF)
    return high, low


def kernel(
    rows, cols, scale,
    head_hbm, cot_hbm, cond_hbm, lx_hbm, ly_hbm, lz_hbm, zmap_hbm, owner_hbm,
    out_ref, zout_ref,
    head, cond, lx, ly, lz, zone_block, zone_turned, zone_y, owner,
    rs, rr, cs, cr, turn, cfx, cfy, cfz_y,
    field0, field3, grad3, grad0, field1, field4, grad4, grad1,
    back5, back2, state2, state5, src_x, src_y,
    zone_cols, zone_lines, lo_x, lo_y, lo_own, hi_own, spread_x, spread_y,
    zacc, z_send, z_mid, z_row, z_col,
    local_sem, rs_sem, rr_sem, cs_sem, cr_sem, zs_sem, zr_sem,
):
    row = lax.axis_index("row")
    col = lax.axis_index("col")
    slab_x, slab_y, depth = head_hbm.shape
    part_x = slab_x // cols
    total_x = lx.shape[0]
    total_y = ly.shape[0]
    half_y = slab_y // 2
    piece_y = half_y // rows

    def row_peer(i):
        return lax.rem(row + i, rows)

    def col_peer(i):
        return lax.rem(col + i, cols)

    loads = {}

    def load(slot, src, dst):
        copy = pltpu.make_async_copy(src, dst, local_sem.at[slot])
        copy.start()
        loads[slot] = copy

    own_x = pl.ds(col * part_x, part_x)
    load(0, cond_hbm, cond)
    load(1, head_hbm, head)
    load(2, cond_hbm.at[own_x], cr.at[0, own_x])
    load(3, cot_hbm.at[own_x], cr.at[1, own_x])
    load(4, lz_hbm, lz)
    load(5, lx_hbm, lx)
    load(6, ly_hbm, ly)
    load(7, zmap_hbm.at[:, pl.ds(pl.multiple_of(col * slab_y, slab_y), slab_y)], zone_block)
    load(8, zmap_hbm.at[pl.ds(row * slab_x + (col * part_x // 8) * 8, 8)], zone_y)
    load(9, owner_hbm, owner)

    barrier = pltpu.get_barrier_semaphore()

    def greet_row(i):
        pl.semaphore_signal(barrier, inc=1, device_id=(row_peer(i + 1), col), device_id_type=MESH)

    def greet_col(i):
        pl.semaphore_signal(barrier, inc=1, device_id=(row, col_peer(i + 1)), device_id_type=MESH)

    loop(rows - 1, greet_row)
    loop(cols - 1, greet_col)

    def near_last(k, count):
        return count // 2 + ((k + 1) // 2) * (1 - 2 * lax.rem(k, 2))

    ring_x = 4
    ring_z = rows // ring_x

    def send_row(k, h):
        def one(shift_z, shift_x):
            z = lax.rem(row // ring_x + shift_z, ring_z)
            x = lax.rem(lax.rem(row, ring_x) + shift_x, ring_x)
            r = z * ring_x + x
            pltpu.make_async_remote_copy(
                src_ref=rs.at[k, h, r], dst_ref=rr.at[k, h, row],
                send_sem=rs_sem.at[k, h], recv_sem=rr_sem.at[k, h],
                device_id=(r, col), device_id_type=MESH,
            ).start()

        shifts_z = [ring_z // 2 + ((i + 1) // 2) * (1 - 2 * (i % 2)) for i in range(ring_z)]

        def lines(i):
            for shift_z in shifts_z:
                one(shift_z, near_last(i, ring_x))

        loop(ring_x - 1, lines)
        for shift_z in shifts_z[:-1]:
            one(shift_z, 0)
        rr[k, h, row] = rs[k, h, row]

    def row_wait(k, h):
        part = pl.ds(0, rows - 1)
        return pltpu.make_async_remote_copy(
            src_ref=rs.at[k, h, part], dst_ref=rr.at[k, h, part],
            send_sem=rs_sem.at[k, h], recv_sem=rr_sem.at[k, h],
            device_id=(row, col), device_id_type=MESH,
        )

    all_y = pl.ds(0, slab_y)

    def half(h):
        return pl.ds(h * half_y, half_y)

    def send_col(j, slot, src, ys):
        def one(i):
            c = col_peer(i + 1)
            pltpu.make_async_remote_copy(
                src_ref=src.at[pl.ds(c * part_x, part_x), ys],
                dst_ref=cr.at[j, own_x, ys],
                send_sem=cs_sem.at[j, slot], recv_sem=cr_sem.at[j, slot],
                device_id=(row, c), device_id_type=MESH,
            ).start()

        loop(cols - 1, one)

    def keep_own(j, src, ys):
        cr[j, own_x, ys] = src[own_x, ys]

    def col_wait(j, slot, ys):
        part = pl.ds(0, (cols - 1) * part_x)
        return pltpu.make_async_remote_copy(
            src_ref=cr.at[j, part, ys], dst_ref=cr.at[j, part, ys],
            send_sem=cs_sem.at[j, slot], recv_sem=cr_sem.at[j, slot],
            device_id=(row, col), device_id_type=MESH,
        )

    def next_lane(f):
        return pltpu.roll(f, f.shape[1] - 1, axis=1)

    def prev_lane(f):
        return pltpu.roll(f, 1, axis=1)

    def apply_z(f, faces):
        flux = faces * (next_lane(f) - f)
        return f + flux - prev_lane(flux)

    def lane_mask(shape):
        lane = lax.broadcasted_iota(jnp.int32, shape, 1)
        return jnp.where(lane < depth - 1, 1.0, 0.0).astype(F32)

    ones8 = jnp.ones((8, 2 * depth), BF)

    def depth_sum(products):
        high, low = split_two(products)
        return dot_nt(ones8, jnp.concatenate([high, low], axis=1))

    def turn_in(x, h, plane):
        turn[pl.ds(h * half_y * slab_x + x, half_y, stride=slab_x), :] = plane

    def turn_out(x, h):
        return turn[pl.ds(h * half_y * slab_x + x, half_y, stride=slab_x), :]

    group = 4
    block = group * piece_y * slab_x

    def turned_to_send(k, h):
        def one(g):
            base = pl.multiple_of(h * half_y * slab_x + g * block, block)
            piece = turn[pl.ds(base, block), :].astype(BF)
            rs[k, h, pl.ds(g * group, group)] = piece.reshape(group, piece_y, slab_x, depth)

        loop(rows // group, one, 2)

    def received_to_turn(k, h):
        def one(g):
            base = pl.multiple_of(h * half_y * slab_x + g * block, block)
            piece = rr[k, h, pl.ds(g * group, group)].reshape(block, depth)
            turn[pl.ds(base, block), :] = piece.astype(F32)

        loop(rows // group, one, 2)

    def received_to_planes(k, h, buf, offset):
        received_to_turn(k, h)

        def one(x):
            buf[offset + x, half(h)] = turn_out(x, h).astype(BF)

        loop(slab_x, one, 4)

    def hub_planes_to_send(buf, k):
        def one(x):
            for h in range(2):
                turn_in(x, h, buf[x, half(h)].astype(F32))

        loop(slab_x, one, 2)
        turned_to_send(k, 0)
        turned_to_send(k, 1)

    def hub_to_lines(k, j, h):
        buf = cs.at[j]
        received_to_planes(k, h, buf, 0)
        send_col(j, h, buf, half(h))
        keep_own(j, buf, half(h))

    chunk = 128
    peers_chunk = chunk // slab_x
    chunks_x = total_x // chunk

    def received_x(k, h, y, c):
        return rr[k, h, pl.ds(c * peers_chunk, peers_chunk), y].reshape(chunk, depth)

    def to_send_x(k, h, y, c, values):
        rs[k, h, pl.ds(c * peers_chunk, peers_chunk), y] = values.astype(BF).reshape(
            peers_chunk, slab_x, depth
        )

    def rows_of(c):
        return pl.ds(pl.multiple_of(PAD + c * chunk, 8), chunk)

    def each_x(body, unroll=1):
        def one(c):
            for y in range(piece_y):
                body(y, c)

        loop(chunks_x, one, unroll)

    def pad_lines_x(field, h):
        for y in range(piece_y):
            pad_line(field, h * piece_y + y, total_x)

    def received_to_field_x(k, h, field):
        def one(y, c):
            field[h * piece_y + y, rows_of(c), :] = received_x(k, h, y, c).astype(F32)

        each_x(one)
        pad_lines_x(field, h)

    def src_part(c):
        return pl.ds(pl.multiple_of(c * chunk, chunk), chunk)

    def forward_x(k_in, k_out, h, field):
        received_to_field_x(k_in, h, field)

        def source(y, c):
            src_x[src_part(c), y * depth:(y + 1) * depth] = apply_lines(
                field, cfx, h * piece_y + y, c
            ).astype(BF)

        each_x(source)

        def line(c):
            res = dot_nn(lx[src_part(c), :], src_x[...])
            for y in range(piece_y):
                to_send_x(k_out, h, y, c, res[:, y * depth:(y + 1) * depth])

        loop(chunks_x, line, 2)
        send_row(k_out, h)

    def adjoint_x(k_in, k_out, h, grad):
        rhs = jnp.concatenate(
            [rr[k_in, h, :, y].reshape(total_x, depth) for y in range(piece_y)], axis=1
        )

        def line(c):
            res = dot_tn(lx[:, src_part(c)], rhs)
            for y in range(piece_y):
                grad[h * piece_y + y, rows_of(c), :] = res[:, y * depth:(y + 1) * depth]

        loop(chunks_x, line, 2)
        pad_lines_x(grad, h)

        def flux(y, c):
            to_send_x(k_out, h, y, c, apply_lines(grad, cfx, h * piece_y + y, c))

        each_x(flux)
        send_row(k_out, h)

    y_chunk = 256
    blocks = y_chunk // slab_y

    def line_y_chunk(m, transpose):
        part = pl.ds(pl.multiple_of(m * y_chunk, y_chunk), y_chunk)
        if transpose:
            return dot_tn(ly[:, part], src_y[...])
        return dot_nn(ly[part, :], src_y[...])

    def line_y_to_field(field):
        def one(m):
            res = line_y_chunk(m, True)
            for x in range(part_x):
                field[x, pl.ds(pl.multiple_of(PAD + m * y_chunk, 8), y_chunk), :] = res[
                    :, x * depth:(x + 1) * depth
                ]

        loop(total_y // y_chunk, one)
        pad_field(field)

    def line_y_to_blocks(body):
        def one(m):
            res = line_y_chunk(m, False).astype(BF)
            for b in range(blocks):
                for x in range(part_x):
                    body(
                        (m * blocks + b) * part_x + x,
                        res[b * slab_y:(b + 1) * slab_y, x * depth:(x + 1) * depth],
                    )

        loop(total_y // y_chunk, one)

    def pad_line(field, line, length):
        field[line, 0:PAD, :] = jnp.broadcast_to(field[line, PAD:PAD + 1, :], (PAD, depth))
        field[line, PAD + length:, :] = jnp.broadcast_to(
            field[line, PAD + length - 1:PAD + length, :], (PAD, depth)
        )

    def pad_field(field):
        for x in range(part_x):
            pad_line(field, x, total_y)

    def received_to_field(j, field):
        def one(c):
            for x in range(part_x):
                field[x, pl.ds(pl.multiple_of(PAD + c * slab_y, 8), slab_y), :] = cr[
                    j, c * part_x + x
                ].astype(F32)

        loop(cols, one, 2)
        pad_field(field)

    def three(field, x, c):
        base = pl.multiple_of(PAD + c * slab_y, 8)
        return (
            field[x, pl.ds(base - 1, slab_y), :],
            field[x, pl.ds(base, slab_y), :],
            field[x, pl.ds(base + 1, slab_y), :],
        )

    def apply_lines(field, faces, x, c):
        below, mid, above = three(field, x, c)
        face_below, face, _ = three(faces, x, c)
        return mid + face * (above - mid) - face_below * (mid - below)

    def apply_y(field, x, c):
        return apply_lines(field, cfy, x, c)

    def cells_line(field, grad, x, c):
        below, mid, above = three(field, x, c)
        g_below, g_mid, g_above = three(grad, x, c)
        return (above - mid) * (g_above - g_mid) + (mid - below) * (g_mid - g_below)

    def faces_line(field, faces, x, c):
        _, mid, above = three(field, x, c)
        faces[x, rows_of(c), :] = HALF_STEP * (mid + above)

    def close_faces(faces, x, length):
        faces[x, 0:PAD, :] = jnp.zeros((PAD, depth), F32)
        faces[x, PAD + length - 1:PAD + length, :] = jnp.zeros((1, depth), F32)
        faces[x, PAD + length:, :] = jnp.zeros((PAD, depth), F32)

    def cells_z(state, backed):
        first = next_lane(state) - state
        second = next_lane(backed) - backed
        return 2.0 * first * second * lane_mask(state.shape)

    def set_src_y(x, c, values):
        src_y[pl.ds(pl.multiple_of(c * slab_y, slab_y), slab_y), x * depth:(x + 1) * depth] = (
            values.astype(BF)
        )

    def source_y(field):
        def one(c):
            for x in range(part_x):
                set_src_y(x, c, apply_y(field, x, c))

        loop(cols, one)

    def low_codes(zones):
        code = jnp.broadcast_to(zones & (depth - 1), (depth, depth))
        return jnp.where(
            code == lax.broadcasted_iota(jnp.int32, (depth, depth), 0), 1.0, 0.0
        ).astype(BF)

    def high_codes(zones):
        code = jnp.broadcast_to(zones // depth, (16, depth))
        return jnp.where(code == lax.broadcasted_iota(jnp.int32, (16, depth), 0), 1.0, 0.0)

    def spread(sums, zones):
        both = jnp.concatenate([sums, sums], axis=0) * high_codes(zones)
        high, low = split_two(both)
        return jnp.concatenate([high, low], axis=0)

    def lanes(index):
        return pl.ds(pl.multiple_of(index * depth, depth), depth)

    def set_codes():
        groups = 8 // part_x
        for x in range(part_x):
            line = jnp.zeros((1, total_y), jnp.int32)
            for g in range(groups):
                mine = jnp.where(lax.rem(col, groups) == g, 1, 0)
                line = line + mine * zone_y[g * part_x + x:g * part_x + x + 1, :]
            for c in range(cols):
                index = c * part_x + x
                zone_lines[index:index + 1, :] = line[:, c * slab_y:(c + 1) * slab_y]
        for c in range(chunks_x):
            block = zone_block[c * chunk:(c + 1) * chunk, :].astype(F32)
            zone_turned[c] = jnp.transpose(block)
        for h in range(2):
            for y in range(piece_y):
                for c in range(chunks_x):
                    index = (h * piece_y + y) * chunks_x + c
                    place = pl.ds(h * half_y + row * piece_y + y, 1)
                    zone_cols[index:index + 1, :] = zone_turned[c, place, :].astype(jnp.int32)

        def one(i):
            lo_x[:, lanes(i)] = low_codes(zone_cols[pl.ds(i, 1), :])
            lo_y[:, lanes(i)] = low_codes(zone_lines[pl.ds(i, 1), :])
            own = owner[pl.ds(i, 1), :]
            lo_own[:, lanes(i)] = low_codes(own)
            hi_own[:, lanes(i)] = high_codes(own)

        loop(16, one)

    def zones_x(field, grad, h):
        def one(c):
            for y in range(piece_y):
                line = h * piece_y + y
                index = line * chunks_x + c
                spread_x[:, lanes(index)] = spread(
                    depth_sum(cells_line(field, grad, line, c)), zone_cols[pl.ds(index, 1), :]
                )

        loop(chunks_x, one, 2)
        count = piece_y * chunks_x * depth
        part = slice(h * count, (h + 1) * count)
        zacc[...] += dot_nt(spread_x[:, part], lo_x[:, part])

    def zones_y():
        def one(c):
            for x in range(part_x):
                index = c * part_x + x
                cells = cells_line(field1, grad1, x, c) + cells_line(field4, grad4, x, c)
                cells = cells + cells_z(state2[index].astype(F32), back2[index])
                cells = cells + cells_z(state5[index].astype(F32), back5[index])
                spread_y[:, lanes(index)] = spread(
                    depth_sum(cells), zone_lines[pl.ds(index, 1), :]
                )

        loop(cols, one)
        zacc[...] += dot_nt(spread_y[...], lo_y[...])

    def back_z(j, back):
        def one(c):
            for x in range(part_x):
                index = c * part_x + x
                backed = dot_nn(cr[j, index], lz[...])
                back[index] = backed
                set_src_y(x, c, apply_z(backed, cfz_y[index]))

        loop(cols, one, 2)

    def back_y(j, grad):
        line_y_to_field(grad)

        def one(c):
            for x in range(part_x):
                cs[j, c * part_x + x] = apply_y(grad, x, c).astype(BF)

        loop(cols, one)
        send_col(j, 0, cs.at[j], all_y)
        keep_own(j, cs.at[j], all_y)

    loads[0].wait()
    hub_planes_to_send(cond, 0)
    loads[1].wait()
    hub_planes_to_send(head, 1)
    pl.semaphore_wait(barrier, rows + cols - 2)
    send_col(1, 0, cot_hbm, all_y)
    send_col(0, 0, cond_hbm, all_y)
    for h in range(2):
        send_row(0, h)
        send_row(1, h)

    for slot in (2, 3, 4, 5, 6):
        loads[slot].wait()
    col_wait(0, 0, all_y).wait_recv()
    received_to_field(0, field1)

    def faces_y(c):
        for x in range(part_x):
            index = c * part_x + x
            own = cr[0, index].astype(F32)
            cfz_y[index] = HALF_STEP * (own + next_lane(own)) * lane_mask(own.shape)
            faces_line(field1, cfy, x, c)

    loop(cols, faces_y)
    for x in range(part_x):
        close_faces(cfy, x, total_y)
    col_wait(1, 0, all_y).wait_recv()
    back_z(1, back5)
    back_y(2, grad4)

    zacc[...] = jnp.zeros(zacc.shape, F32)
    for h in range(2):
        row_wait(0, h).wait_recv()
        received_to_field_x(0, h, field3)

        def faces_x(y, c):
            faces_line(field3, cfx, h * piece_y + y, c)

        each_x(faces_x)
        for y in range(piece_y):
            close_faces(cfx, h * piece_y + y, total_x)
        row_wait(1, h).wait_recv()
        forward_x(1, 2, h, field0)
    for slot in (7, 8, 9):
        loads[slot].wait()
    set_codes()

    col_wait(2, 0, all_y).wait_recv()
    hub_planes_to_send(cr.at[2], 3)
    for h in range(2):
        row_wait(2, h).wait_recv()
        send_row(3, h)
        hub_to_lines(2, 3, h)

    row_wait(3, 0).wait_recv()
    adjoint_x(3, 4, 0, grad3)

    for h in range(2):
        col_wait(3, h, half(h)).wait_recv()
    received_to_field(3, field1)
    source_y(field1)

    def state3_block(index, state):
        state2[index] = state
        source = apply_z(state.astype(F32), cfz_y[index]).astype(BF)
        cs[4, index] = dot_nt(source, lz[...]).astype(BF)

    line_y_to_blocks(state3_block)
    send_col(4, 0, cs.at[4], all_y)
    keep_own(4, cs.at[4], all_y)

    row_wait(3, 1).wait_recv()
    adjoint_x(3, 4, 1, grad3)
    col_wait(4, 0, all_y).wait_recv()
    hub_planes_to_send(cr.at[4], 5)

    for h in range(2):
        row_wait(4, h).wait_recv()
        send_row(5, h)
        hub_to_lines(4, 5, h)

    row_wait(5, 0).wait_recv()
    forward_x(5, 6, 0, field3)

    for h in range(2):
        col_wait(5, h, half(h)).wait_recv()
    back_z(5, back2)
    back_y(6, grad1)

    row_wait(5, 1).wait_recv()
    forward_x(5, 6, 1, field3)
    zones_x(field3, grad3, 0)
    zones_x(field3, grad3, 1)
    col_wait(6, 0, all_y).wait_recv()
    hub_planes_to_send(cr.at[6], 7)

    for h in range(2):
        row_wait(6, h).wait_recv()
        send_row(7, h)
        hub_to_lines(6, 7, h)

    row_wait(7, 0).wait_recv()
    adjoint_x(7, 8, 0, grad0)

    for h in range(2):
        col_wait(7, h, half(h)).wait_recv()
    received_to_field(7, field4)
    source_y(field4)

    def state5_block(index, state):
        state5[index] = state

    line_y_to_blocks(state5_block)
    zones_y()
    zones_x(field0, grad0, 0)

    row_wait(7, 1).wait_recv()
    adjoint_x(7, 8, 1, grad0)
    zones_x(field0, grad0, 1)

    sums = (zacc[0:16, :] + zacc[16:32, :]) * (-HALF_STEP * scale)
    high, low = split_two(sums)
    ordered = dot_nn(jnp.concatenate([high, low], axis=0), lo_own[...])
    ordered = (ordered[0:16] + ordered[16:32]) * hi_own[...]
    ordered = jnp.sum(ordered, axis=0, keepdims=True)
    for g in range(z_send.shape[0]):
        z_send[g] = jnp.broadcast_to(ordered[:, g * depth:(g + 1) * depth], (8, depth))

    def send_zone_row(i):
        r = row_peer(i + 1)
        pltpu.make_async_remote_copy(
            src_ref=z_send.at[r // 2], dst_ref=z_row.at[row],
            send_sem=zs_sem.at[0], recv_sem=zr_sem.at[0],
            device_id=(r, col), device_id_type=MESH,
        ).start()

    loop(rows - 1, send_zone_row)
    z_row[row] = z_send[row // 2]
    row_wait(8, 0).wait_recv()
    received_to_planes(8, 0, out_ref, 0)

    def zone_wait(phase, ref, count):
        part = pl.ds(0, count)
        return pltpu.make_async_remote_copy(
            src_ref=ref.at[part], dst_ref=ref.at[part],
            send_sem=zs_sem.at[phase], recv_sem=zr_sem.at[phase],
            device_id=(row, col), device_id_type=MESH,
        )

    zone_wait(0, z_row, rows - 1).wait_recv()
    z_mid[...] = jnp.sum(z_row[...], axis=0)

    def send_zone_col(i):
        c = col_peer(i + 1)
        pltpu.make_async_remote_copy(
            src_ref=z_mid, dst_ref=z_col.at[col],
            send_sem=zs_sem.at[1], recv_sem=zr_sem.at[1],
            device_id=(row, c), device_id_type=MESH,
        ).start()

    loop(cols - 1, send_zone_col)
    z_col[col] = z_mid[...]
    row_wait(8, 1).wait_recv()
    received_to_planes(8, 1, out_ref, 0)
    zone_wait(1, z_col, cols - 1).wait_recv()
    final = jnp.sum(z_col[...], axis=0)
    offset = lax.rem(row, 2) * (depth // 2) + col * 8
    zout_ref[...] = pltpu.roll(final, lax.rem(depth - offset, depth), axis=1)

    for k in range(9):
        for h in range(2):
            row_wait(k, h).wait_send()
    for j in (0, 1, 2, 4, 6):
        col_wait(j, 0, all_y).wait_send()
    for j in (3, 5, 7):
        for h in range(2):
            col_wait(j, h, half(h)).wait_send()
    zone_wait(0, z_row, rows - 1).wait_send()
    zone_wait(1, z_col, cols - 1).wait_send()


def on_device(
    rows, cols, head_start, cotangent, conductivity, line_x, line_y, line_z, zone_map, owner_order
):
    slab_x, slab_y, depth = head_start.shape
    total_x, total_y = zone_map.shape
    zone_count = owner_order.shape[0]
    part_x = slab_x // cols
    part_y = slab_y // rows
    scale = 1.0 / math.sqrt(total_x * total_y * depth / zone_count)
    groups = zone_count // depth
    lines_x = pltpu.VMEM((part_y, total_x + 2 * PAD, depth), F32)
    lines_y = pltpu.VMEM((part_x, total_y + 2 * PAD, depth), F32)
    slab16 = pltpu.VMEM((slab_x, slab_y, depth), BF)
    slab32 = pltpu.VMEM((slab_x, slab_y, depth), F32)
    codes = pltpu.VMEM((depth, slab_x * slab_y), BF)
    spread = pltpu.VMEM((32, slab_x * slab_y), BF)
    row_slots = pltpu.VMEM((9, 2, rows, part_y // 2, slab_x, depth), BF)
    col_slots = pltpu.VMEM((8, slab_x, slab_y, depth), BF)
    scratch = [
        slab16, slab16,
        pltpu.VMEM(line_x.shape, BF),
        pltpu.VMEM(line_y.shape, BF),
        pltpu.VMEM(line_z.shape, BF),
        pltpu.VMEM((total_x, slab_y), jnp.int32),
        pltpu.VMEM((total_x // 128, slab_y, 128), F32),
        pltpu.VMEM((8, total_y), jnp.int32),
        pltpu.VMEM((groups, depth), jnp.int32),
        row_slots, row_slots, col_slots, col_slots,
        pltpu.VMEM((slab_x * slab_y, depth), F32),
        lines_x, lines_y, slab32,
        lines_x, lines_x, lines_x, lines_x,
        lines_y, lines_y, lines_y, lines_y,
        slab32, slab32, slab16, slab16,
        pltpu.VMEM((total_x, part_y // 2 * depth), BF),
        pltpu.VMEM((total_y, part_x * depth), BF),
        pltpu.VMEM((16, depth), jnp.int32),
        pltpu.VMEM((16, depth), jnp.int32),
        codes, codes, codes,
        pltpu.VMEM((16, zone_count), F32),
        spread, spread,
        pltpu.VMEM((32, depth), F32),
        pltpu.VMEM((groups, 8, depth), F32),
        pltpu.VMEM((8, depth), F32),
        pltpu.VMEM((rows, 8, depth), F32),
        pltpu.VMEM((cols, 8, depth), F32),
        pltpu.SemaphoreType.DMA((10,)),
        pltpu.SemaphoreType.DMA((9, 2)),
        pltpu.SemaphoreType.DMA((9, 2)),
        pltpu.SemaphoreType.DMA((8, 2)),
        pltpu.SemaphoreType.DMA((8, 2)),
        pltpu.SemaphoreType.DMA((2,)),
        pltpu.SemaphoreType.DMA((2,)),
    ]
    adjoint, zones = pl.pallas_call(
        functools.partial(kernel, rows, cols, scale),
        out_shape=(
            jax.ShapeDtypeStruct((slab_x, slab_y, depth), BF),
            jax.ShapeDtypeStruct((8, depth), F32),
        ),
        in_specs=[pl.BlockSpec(memory_space=pl.ANY)] * 8,
        out_specs=(
            pl.BlockSpec(memory_space=pltpu.VMEM),
            pl.BlockSpec(memory_space=pltpu.VMEM),
        ),
        scratch_shapes=scratch,
        compiler_params=pltpu.CompilerParams(
            collective_id=0, has_side_effects=True, vmem_limit_bytes=56 << 20
        ),
        name="adjoint_lines",
    )(
        head_start, cotangent, conductivity, line_x, line_y, line_z, zone_map,
        owner_order.reshape(groups, depth),
    )
    return adjoint, zones[0, : zone_count // (rows * cols)]


def solution(mesh):
    slab = P("row", "col", None)
    return jax.shard_map(
        functools.partial(on_device, mesh.shape["row"], mesh.shape["col"]),
        mesh=mesh,
        in_specs=(slab, slab, slab, P(), P(), P(), P(), P()),
        out_specs=(slab, P(("row", "col"))),
        check_vma=False,
    )
```

time: 566 us -> 128 us (0.23); the launches traced: 555 us -> 128 us
  blocking collectives: 126 us -> 0 us
  Pallas kernels: 0 us -> 124 us
  other arithmetic: 117 us -> 0 us
  waiting for transfers between devices: 113 us -> 0 us
  starting transfers between devices: 93.7 us -> 0 us
  local copies, waits for them, and re-layouts: 84.6 us -> 3.07 us
  matrix products: 20 us -> 0 us
    pallas_call x0 -> x1, Pallas kernels: none -> 124 us  [on_device(): pl.pallas_call(functools.partial(kernel, rows, cols, scale), out_shape=(j...]
    all_to_all x15 -> x0, waiting for transfers between devices: 113 us -> none  [the longest x2 28.4 us: to_lines(): return lax.all_to_all(heads, 'row', split_axis=1, concat_axis=0, tiled=True)]
    all_to_all x15 -> x0, starting transfers between devices: 93.7 us -> none  [the longest x3 19.6 us: from_lines(): return lax.all_to_all(heads, 'col', split_axis=1, concat_axis=0, tiled=True)]
    unnamed x1 -> x0, blocking collectives: 75.1 us -> none
    scatter-add x6 -> x0, other arithmetic: 68.8 us -> none  [on_device(): jax.ops.segment_sum(column_grad.reshape(-1), zone_ids[direction].reshape(...]
    all_to_all x3 -> x0, blocking collectives: 50.5 us -> none  [the longest x1 21.3 us: from_lines(): return lax.all_to_all(heads, 'row', split_axis=0, concat_axis=1, tiled=True)]
    convert_element_type x22 -> x0, local copies, waits for them, and re-layouts: 37.3 us -> none  [the longest x7 13.3 us: on_device(): widened = line_field.astype(jnp.float32)]
    mul x10 -> x0, other arithmetic: 21.5 us -> none  [the longest x5 14 us: flux_product(): jnp.diff(states, axis=direction) * jnp.diff(backed, axis=direction)]
  transfers between devices with their start and end apart: 15 -> 0, of which waited for: 13 -> 0; matrix products, arithmetic and copies ran while one was open for 21% -> 0% of each run, Pallas kernels for 0% -> 0%
where the time goes in v2:
time: 128 us
  Pallas kernels  124 us (97%)
  local copies, waits for them, and re-layouts  3.07 us (2%)
    pallas_call x1, Pallas kernels, on_device(): pl.pallas_call(functools.partial(kernel, rows, cols, scale), out_shape=(j...  124 us

profile of v2, /device:TPU:1, one launch (start us, length us, event | category | flops | bytes accessed | tf_op | source)
XLA Modules:
  0.0 127.7 jit_solution(13163333766080655952)
XLA Ops:
  0.6 124.0 %adjoint_lines.1 = (bf16[16,128,128]{2,1,0:T(8,128)(2,1)}, f32[8,128]{1,0:T(8,128)}) custom-call(bf16[16,128,128]{2,1,0:T(8,128)(2,1)} %head_hbm.1, bf16[16,128,128]{2,1,0:T(8,128)(2,1)} %cot_hbm.1, bf16[16,128,128]{2,1,0:T(8,128)(2,1)} %cond_hbm.1, bf16[512,512]{1,0:T(8,128)(2,1)} %lx_hbm.1, bf16[1024,1024]{1,0:T(8,128)(2,1)} %ly_hbm.1, ...), custom_call_target="tpu_custom_call" | custom-call | tf_op jit(solution)/shard_map/adjoint_lines/pallas_call | solution.py:735
  124.6 1.2 slice_bitcast_fusion
  125.8 1.9 %copy.11 = bf16[16,128,128]{2,1,0:T(8,128)(2,1)} copy(bf16[16,128,128]{2,1,0:T(8,128)(2,1)} %get-tuple-element.8) | data formatting | bytes 1048576

commit v3 on v2

--- a/solution.py
+++ b/solution.py
@@ -78,6 +78,17 @@
     own_x = pl.ds(col * part_x, part_x)
     load(0, cond_hbm, cond)
     load(1, head_hbm, head)
+
+    barrier = pltpu.get_barrier_semaphore()
+
+    def greet_row(i):
+        pl.semaphore_signal(barrier, inc=1, device_id=(row_peer(i + 1), col), device_id_type=MESH)
+
+    def greet_col(i):
+        pl.semaphore_signal(barrier, inc=1, device_id=(row, col_peer(i + 1)), device_id_type=MESH)
+
+    loop(rows - 1, greet_row)
+    loop(cols - 1, greet_col)
     load(2, cond_hbm.at[own_x], cr.at[0, own_x])
     load(3, cot_hbm.at[own_x], cr.at[1, own_x])
     load(4, lz_hbm, lz)
@@ -87,27 +98,17 @@
     load(8, zmap_hbm.at[pl.ds(row * slab_x + (col * part_x // 8) * 8, 8)], zone_y)
     load(9, owner_hbm, owner)
 
-    barrier = pltpu.get_barrier_semaphore()
-
-    def greet_row(i):
-        pl.semaphore_signal(barrier, inc=1, device_id=(row_peer(i + 1), col), device_id_type=MESH)
-
-    def greet_col(i):
-        pl.semaphore_signal(barrier, inc=1, device_id=(row, col_peer(i + 1)), device_id_type=MESH)
-
-    loop(rows - 1, greet_row)
-    loop(cols - 1, greet_col)
-
     def near_last(k, count):
         return count // 2 + ((k + 1) // 2) * (1 - 2 * lax.rem(k, 2))
 
     ring_x = 4
+    side = lax.rem(col, 2)
     ring_z = rows // ring_x
 
     def send_row(k, h):
         def one(shift_z, shift_x):
-            z = lax.rem(row // ring_x + shift_z, ring_z)
-            x = lax.rem(lax.rem(row, ring_x) + shift_x, ring_x)
+            z = lax.rem(row // ring_x + shift_z + side * (ring_z - 2 * shift_z), ring_z)
+            x = lax.rem(lax.rem(row, ring_x) + shift_x + side * (ring_x - 2 * shift_x), ring_x)
             r = z * ring_x + x
             pltpu.make_async_remote_copy(
                 src_ref=rs.at[k, h, r], dst_ref=rr.at[k, h, row],
@@ -215,14 +216,16 @@
 
         loop(slab_x, one, 4)
 
+    def half_planes_to_send(buf, k, h):
+        def one(x):
+            turn_in(x, h, buf[x, half(h)].astype(F32))
+
+        loop(slab_x, one, 4)
+        turned_to_send(k, h)
+
     def hub_planes_to_send(buf, k):
-        def one(x):
-            for h in range(2):
-                turn_in(x, h, buf[x, half(h)].astype(F32))
-
-        loop(slab_x, one, 2)
-        turned_to_send(k, 0)
-        turned_to_send(k, 1)
+        for h in range(2):
+            half_planes_to_send(buf, k, h)
 
     def hub_to_lines(k, j, h):
         buf = cs.at[j]
@@ -284,7 +287,7 @@
         loop(chunks_x, line, 2)
         send_row(k_out, h)
 
-    def adjoint_x(k_in, k_out, h, grad):
+    def back_x(k_in, h, grad):
         rhs = jnp.concatenate(
             [rr[k_in, h, :, y].reshape(total_x, depth) for y in range(piece_y)], axis=1
         )
@@ -297,11 +300,16 @@
         loop(chunks_x, line, 2)
         pad_lines_x(grad, h)
 
+    def flux_x(k_out, h, grad):
         def flux(y, c):
             to_send_x(k_out, h, y, c, apply_lines(grad, cfx, h * piece_y + y, c))
 
         each_x(flux)
         send_row(k_out, h)
+
+    def adjoint_x(k_in, k_out, h, grad):
+        back_x(k_in, h, grad)
+        flux_x(k_out, h, grad)
 
     y_chunk = 256
     blocks = y_chunk // slab_y
@@ -463,13 +471,12 @@
         part = slice(h * count, (h + 1) * count)
         zacc[...] += dot_nt(spread_x[:, part], lo_x[:, part])
 
-    def zones_y():
+    def zones_y(field, grad, state, back):
         def one(c):
             for x in range(part_x):
                 index = c * part_x + x
-                cells = cells_line(field1, grad1, x, c) + cells_line(field4, grad4, x, c)
-                cells = cells + cells_z(state2[index].astype(F32), back2[index])
-                cells = cells + cells_z(state5[index].astype(F32), back5[index])
+                cells = cells_line(field, grad, x, c)
+                cells = cells + cells_z(state[index].astype(F32), back[index])
                 spread_y[:, lanes(index)] = spread(
                     depth_sum(cells), zone_lines[pl.ds(index, 1), :]
                 )
@@ -499,15 +506,18 @@
         keep_own(j, cs.at[j], all_y)
 
     loads[0].wait()
-    hub_planes_to_send(cond, 0)
+    half_planes_to_send(cond, 0, 0)
+    pl.semaphore_wait(barrier, rows + cols - 2)
+    send_row(0, 0)
     loads[1].wait()
-    hub_planes_to_send(head, 1)
-    pl.semaphore_wait(barrier, rows + cols - 2)
+    half_planes_to_send(head, 1, 0)
+    send_row(1, 0)
+    send_col(0, 0, cond_hbm, all_y)
     send_col(1, 0, cot_hbm, all_y)
-    send_col(0, 0, cond_hbm, all_y)
-    for h in range(2):
-        send_row(0, h)
-        send_row(1, h)
+    half_planes_to_send(cond, 0, 1)
+    send_row(0, 1)
+    half_planes_to_send(head, 1, 1)
+    send_row(1, 1)
 
     for slot in (2, 3, 4, 5, 6):
         loads[slot].wait()
@@ -598,9 +608,11 @@
         row_wait(6, h).wait_recv()
         send_row(7, h)
         hub_to_lines(6, 7, h)
+    zones_y(field1, grad1, state2, back2)
 
     row_wait(7, 0).wait_recv()
     adjoint_x(7, 8, 0, grad0)
+    zones_x(field0, grad0, 0)
 
     for h in range(2):
         col_wait(7, h, half(h)).wait_recv()
@@ -611,11 +623,10 @@
         state5[index] = state
 
     line_y_to_blocks(state5_block)
-    zones_y()
-    zones_x(field0, grad0, 0)
+    zones_y(field4, grad4, state5, back5)
 
     row_wait(7, 1).wait_recv()
-    adjoint_x(7, 8, 1, grad0)
+    back_x(7, 1, grad0)
     zones_x(field0, grad0, 1)
 
     sums = (zacc[0:16, :] + zacc[16:32, :]) * (-HALF_STEP * scale)
@@ -624,7 +635,7 @@
     ordered = (ordered[0:16] + ordered[16:32]) * hi_own[...]
     ordered = jnp.sum(ordered, axis=0, keepdims=True)
     for g in range(z_send.shape[0]):
-        z_send[g] = jnp.broadcast_to(ordered[:, g * depth:(g + 1) * depth], (8, depth))
+        z_send[g] = ordered[:, g * depth:(g + 1) * depth]
 
     def send_zone_row(i):
         r = row_peer(i + 1)
@@ -636,8 +647,7 @@
 
     loop(rows - 1, send_zone_row)
     z_row[row] = z_send[row // 2]
-    row_wait(8, 0).wait_recv()
-    received_to_planes(8, 0, out_ref, 0)
+    flux_x(8, 1, grad0)
 
     def zone_wait(phase, ref, count):
         part = pl.ds(0, count)
@@ -660,12 +670,15 @@
 
     loop(cols - 1, send_zone_col)
     z_col[col] = z_mid[...]
-    row_wait(8, 1).wait_recv()
-    received_to_planes(8, 1, out_ref, 0)
+    row_wait(8, 0).wait_recv()
+    out_ref[0] = rr[8, 0]
     zone_wait(1, z_col, cols - 1).wait_recv()
     final = jnp.sum(z_col[...], axis=0)
     offset = lax.rem(row, 2) * (depth // 2) + col * 8
+    final = jnp.broadcast_to(final, zout_ref.shape)
     zout_ref[...] = pltpu.roll(final, lax.rem(depth - offset, depth), axis=1)
+    row_wait(8, 1).wait_recv()
+    out_ref[1] = rr[8, 1]
 
     for k in range(9):
         for h in range(2):
@@ -677,6 +690,18 @@
             col_wait(j, h, half(h)).wait_send()
     zone_wait(0, z_row, rows - 1).wait_send()
     zone_wait(1, z_col, cols - 1).wait_send()
+
+
+def finish(turned_ref, zones_ref, out_ref, zout_ref, turn):
+    slab_x, slab_y, depth = out_ref.shape
+    count = slab_x * slab_y
+    turn[...] = turned_ref[...].reshape(count, depth).astype(F32)
+
+    def one(x):
+        out_ref[x] = turn[pl.ds(x, slab_y, stride=slab_x), :].astype(BF)
+
+    loop(slab_x, one, 4)
+    zout_ref[...] = zones_ref[0, 0:zout_ref.shape[0]]
 
 
 def on_device(
@@ -720,10 +745,10 @@
         pltpu.VMEM((16, zone_count), F32),
         spread, spread,
         pltpu.VMEM((32, depth), F32),
-        pltpu.VMEM((groups, 8, depth), F32),
-        pltpu.VMEM((8, depth), F32),
-        pltpu.VMEM((rows, 8, depth), F32),
-        pltpu.VMEM((cols, 8, depth), F32),
+        pltpu.VMEM((groups, 1, depth), F32),
+        pltpu.VMEM((1, depth), F32),
+        pltpu.VMEM((rows, 1, depth), F32),
+        pltpu.VMEM((cols, 1, depth), F32),
         pltpu.SemaphoreType.DMA((10,)),
         pltpu.SemaphoreType.DMA((9, 2)),
         pltpu.SemaphoreType.DMA((9, 2)),
@@ -732,10 +757,10 @@
         pltpu.SemaphoreType.DMA((2,)),
         pltpu.SemaphoreType.DMA((2,)),
     ]
-    adjoint, zones = pl.pallas_call(
+    turned, zones = pl.pallas_call(
         functools.partial(kernel, rows, cols, scale),
         out_shape=(
-            jax.ShapeDtypeStruct((slab_x, slab_y, depth), BF),
+            jax.ShapeDtypeStruct((2, rows, part_y // 2, slab_x, depth), BF),
             jax.ShapeDtypeStruct((8, depth), F32),
         ),
         in_specs=[pl.BlockSpec(memory_space=pl.ANY)] * 8,
@@ -752,7 +777,18 @@
         head_start, cotangent, conductivity, line_x, line_y, line_z, zone_map,
         owner_order.reshape(groups, depth),
     )
-    return adjoint, zones[0, : zone_count // (rows * cols)]
+    vmem = pl.BlockSpec(memory_space=pltpu.VMEM)
+    return pl.pallas_call(
+        finish,
+        out_shape=(
+            jax.ShapeDtypeStruct((slab_x, slab_y, depth), BF),
+            jax.ShapeDtypeStruct((zone_count // (rows * cols),), F32),
+        ),
+        in_specs=[vmem, vmem],
+        out_specs=(vmem, vmem),
+        scratch_shapes=[pltpu.VMEM((slab_x * slab_y, depth), F32)],
+        name="finish_slab",
+    )(turned, zones)
 
 
 def solution(mesh):

time: 128 us -> 121 us (0.945)
  Pallas kernels: 124 us -> 120 us
  local copies, waits for them, and re-layouts: 3.07 us -> 0 us
    pallas_call x1, Pallas kernels: 124 us -> 118 us  [on_device(): pl.pallas_call(functools.partial(kernel, rows, cols, scale), out_shape=(j...]
    pallas_call x0 -> x1, Pallas kernels: none -> 2.29 us  [on_device(): pl.pallas_call(finish, out_shape=(jax.ShapeDtypeStruct((slab_x, slab_y, d...]
    unnamed x1 -> x0, local copies, waits for them, and re-layouts: 1.88 us -> none
where the time goes in v3:
time: 121 us
  Pallas kernels  120 us (99%)
    pallas_call x1, Pallas kernels, on_device(): pl.pallas_call(functools.partial(kernel, rows, cols, scale), out_shape=(j...  118 us

profile of v3, /device:TPU:1, one launch (start us, length us, event | category | flops | bytes accessed | tf_op | source)
XLA Modules:
  0.0 120.6 jit_solution(15000166133231060238)
XLA Ops:
  0.6 117.7 %adjoint_lines.1 = (bf16[2,32,2,16,128]{4,3,2,1,0:T(8,128)(2,1)}, f32[8,128]{1,0:T(8,128)}) custom-call(bf16[16,128,128]{2,1,0:T(8,128)(2,1)} %head_hbm.1, bf16[16,128,128]{2,1,0:T(8,128)(2,1)} %cot_hbm.1, bf16[16,128,128]{2,1,0:T(8,128)(2,1)} %cond_hbm.1, bf16[512,512]{1,0:T(8,128)(2,1)} %lx_hbm.1, bf16[1024,1024]{1,0:T(8,128)(2,1)} %ly_hbm.1, ...), custom_call_target="tpu_custom_call" | custom-call | tf_op jit(solution)/shard_map/adjoint_lines/pallas_call | solution.py:760
  118.3 2.3 %finish_slab.1 = (bf16[16,128,128]{2,1,0:T(8,128)(2,1)}, f32[8]{0:T(128)}) custom-call(bf16[2,32,2,16,128]{4,3,2,1,0:T(8,128)(2,1)} %get-tuple-element.4.turned_ref, f32[8,128]{1,0:T(8,128)} %get-tuple-element.5.zones_ref), custom_call_target="tpu_custom_call" | custom-call | tf_op jit(solution)/shard_map/finish_slab/pallas_call | solution.py:781

commit v4 on v3

--- a/solution.py
+++ b/solution.py
@@ -68,6 +68,17 @@
     def col_peer(i):
         return lax.rem(col + i, cols)
 
+    barrier = pltpu.get_barrier_semaphore()
+
+    def greet_row(i):
+        pl.semaphore_signal(barrier, inc=1, device_id=(row_peer(i + 1), col), device_id_type=MESH)
+
+    def greet_col(i):
+        pl.semaphore_signal(barrier, inc=1, device_id=(row, col_peer(i + 1)), device_id_type=MESH)
+
+    loop(rows - 1, greet_row, rows - 1)
+    loop(cols - 1, greet_col, cols - 1)
+
     loads = {}
 
     def load(slot, src, dst):
@@ -78,25 +89,6 @@
     own_x = pl.ds(col * part_x, part_x)
     load(0, cond_hbm, cond)
     load(1, head_hbm, head)
-
-    barrier = pltpu.get_barrier_semaphore()
-
-    def greet_row(i):
-        pl.semaphore_signal(barrier, inc=1, device_id=(row_peer(i + 1), col), device_id_type=MESH)
-
-    def greet_col(i):
-        pl.semaphore_signal(barrier, inc=1, device_id=(row, col_peer(i + 1)), device_id_type=MESH)
-
-    loop(rows - 1, greet_row)
-    loop(cols - 1, greet_col)
-    load(2, cond_hbm.at[own_x], cr.at[0, own_x])
-    load(3, cot_hbm.at[own_x], cr.at[1, own_x])
-    load(4, lz_hbm, lz)
-    load(5, lx_hbm, lx)
-    load(6, ly_hbm, ly)
-    load(7, zmap_hbm.at[:, pl.ds(pl.multiple_of(col * slab_y, slab_y), slab_y)], zone_block)
-    load(8, zmap_hbm.at[pl.ds(row * slab_x + (col * part_x // 8) * 8, 8)], zone_y)
-    load(9, owner_hbm, owner)
 
     def near_last(k, count):
         return count // 2 + ((k + 1) // 2) * (1 - 2 * lax.rem(k, 2))
@@ -512,6 +504,14 @@
     loads[1].wait()
     half_planes_to_send(head, 1, 0)
     send_row(1, 0)
+    load(2, cond_hbm.at[own_x], cr.at[0, own_x])
+    load(3, cot_hbm.at[own_x], cr.at[1, own_x])
+    load(4, lz_hbm, lz)
+    load(5, lx_hbm, lx)
+    load(6, ly_hbm, ly)
+    load(7, zmap_hbm.at[:, pl.ds(pl.multiple_of(col * slab_y, slab_y), slab_y)], zone_block)
+    load(8, zmap_hbm.at[pl.ds(row * slab_x + (col * part_x // 8) * 8, 8)], zone_y)
+    load(9, owner_hbm, owner)
     send_col(0, 0, cond_hbm, all_y)
     send_col(1, 0, cot_hbm, all_y)
     half_planes_to_send(cond, 0, 1)
@@ -629,6 +629,10 @@
     back_x(7, 1, grad0)
     zones_x(field0, grad0, 1)
 
+    def leave(h):
+        received_to_planes(8, h, cs.at[0], 0)
+        load(10 + h, cs.at[0, :, half(h)], out_ref.at[:, half(h)])
+
     sums = (zacc[0:16, :] + zacc[16:32, :]) * (-HALF_STEP * scale)
     high, low = split_two(sums)
     ordered = dot_nn(jnp.concatenate([high, low], axis=0), lo_own[...])
@@ -671,14 +675,16 @@
     loop(cols - 1, send_zone_col)
     z_col[col] = z_mid[...]
     row_wait(8, 0).wait_recv()
-    out_ref[0] = rr[8, 0]
+    leave(0)
     zone_wait(1, z_col, cols - 1).wait_recv()
     final = jnp.sum(z_col[...], axis=0)
     offset = lax.rem(row, 2) * (depth // 2) + col * 8
     final = jnp.broadcast_to(final, zout_ref.shape)
     zout_ref[...] = pltpu.roll(final, lax.rem(depth - offset, depth), axis=1)
     row_wait(8, 1).wait_recv()
-    out_ref[1] = rr[8, 1]
+    leave(1)
+    for h in range(2):
+        loads[10 + h].wait()
 
     for k in range(9):
         for h in range(2):
@@ -692,15 +698,8 @@
     zone_wait(1, z_col, cols - 1).wait_send()
 
 
-def finish(turned_ref, zones_ref, out_ref, zout_ref, turn):
-    slab_x, slab_y, depth = out_ref.shape
-    count = slab_x * slab_y
-    turn[...] = turned_ref[...].reshape(count, depth).astype(F32)
-
-    def one(x):
-        out_ref[x] = turn[pl.ds(x, slab_y, stride=slab_x), :].astype(BF)
-
-    loop(slab_x, one, 4)
+def finish(slab_ref, zones_ref, out_ref, zout_ref):
+    out_ref[...] = slab_ref[...]
     zout_ref[...] = zones_ref[0, 0:zout_ref.shape[0]]
 
 
@@ -732,7 +731,7 @@
         pltpu.VMEM((8, total_y), jnp.int32),
         pltpu.VMEM((groups, depth), jnp.int32),
         row_slots, row_slots, col_slots, col_slots,
-        pltpu.VMEM((slab_x * slab_y, depth), F32),
+        pltpu.VMEM((slab_x * slab_y + slab_x, depth), F32),
         lines_x, lines_y, slab32,
         lines_x, lines_x, lines_x, lines_x,
         lines_y, lines_y, lines_y, lines_y,
@@ -749,7 +748,7 @@
         pltpu.VMEM((1, depth), F32),
         pltpu.VMEM((rows, 1, depth), F32),
         pltpu.VMEM((cols, 1, depth), F32),
-        pltpu.SemaphoreType.DMA((10,)),
+        pltpu.SemaphoreType.DMA((12,)),
         pltpu.SemaphoreType.DMA((9, 2)),
         pltpu.SemaphoreType.DMA((9, 2)),
         pltpu.SemaphoreType.DMA((8, 2)),
@@ -760,12 +759,12 @@
     turned, zones = pl.pallas_call(
         functools.partial(kernel, rows, cols, scale),
         out_shape=(
-            jax.ShapeDtypeStruct((2, rows, part_y // 2, slab_x, depth), BF),
+            jax.ShapeDtypeStruct((slab_x, slab_y, depth), BF),
             jax.ShapeDtypeStruct((8, depth), F32),
         ),
         in_specs=[pl.BlockSpec(memory_space=pl.ANY)] * 8,
         out_specs=(
-            pl.BlockSpec(memory_space=pltpu.VMEM),
+            pl.BlockSpec(memory_space=pl.ANY),
             pl.BlockSpec(memory_space=pltpu.VMEM),
         ),
         scratch_shapes=scratch,
@@ -786,7 +785,6 @@
         ),
         in_specs=[vmem, vmem],
         out_specs=(vmem, vmem),
-        scratch_shapes=[pltpu.VMEM((slab_x * slab_y, depth), F32)],
         name="finish_slab",
     )(turned, zones)
 

time: 121 us -> 121 us (level)
  no operation moved by 1% of the time
where the time goes in v4:
time: 121 us
  Pallas kernels  120 us (99%)
    pallas_call x1, Pallas kernels, on_device(): pl.pallas_call(functools.partial(kernel, rows, cols, scale), out_shape=(j...  118 us

profile of v4, /device:TPU:1, one launch (start us, length us, event | category | flops | bytes accessed | tf_op | source)
XLA Modules:
  0.0 120.9 jit_solution(772170476181015638)
XLA Ops:
  0.6 118.4 %adjoint_lines.1 = (bf16[16,128,128]{2,1,0:T(8,128)(2,1)}, f32[8,128]{1,0:T(8,128)}) custom-call(bf16[16,128,128]{2,1,0:T(8,128)(2,1)} %head_hbm.1, bf16[16,128,128]{2,1,0:T(8,128)(2,1)} %cot_hbm.1, bf16[16,128,128]{2,1,0:T(8,128)(2,1)} %cond_hbm.1, bf16[512,512]{1,0:T(8,128)(2,1)} %lx_hbm.1, bf16[1024,1024]{1,0:T(8,128)(2,1)} %ly_hbm.1, ...), custom_call_target="tpu_custom_call" | custom-call | tf_op jit(solution)/shard_map/adjoint_lines/pallas_call | solution.py:759
  119.0 1.9 %finish_slab.1 = (bf16[16,128,128]{2,1,0:T(8,128)(2,1)}, f32[8]{0:T(128)}) custom-call(bf16[16,128,128]{2,1,0:T(8,128)(2,1)} %get-tuple-element.4.slab_ref, f32[8,128]{1,0:T(8,128)} %get-tuple-element.5.zones_ref), custom_call_target="tpu_custom_call" | custom-call | tf_op jit(solution)/shard_map/finish_slab/pallas_call | solution.py:780

commit v5 on v4

--- a/solution.py
+++ b/solution.py
@@ -400,7 +400,7 @@
             for x in range(part_x):
                 set_src_y(x, c, apply_y(field, x, c))
 
-        loop(cols, one)
+        loop(cols, one, 2)
 
     def low_codes(zones):
         code = jnp.broadcast_to(zones & (depth - 1), (depth, depth))
@@ -458,7 +458,7 @@
                     depth_sum(cells_line(field, grad, line, c)), zone_cols[pl.ds(index, 1), :]
                 )
 
-        loop(chunks_x, one, 2)
+        loop(chunks_x, one, 4)
         count = piece_y * chunks_x * depth
         part = slice(h * count, (h + 1) * count)
         zacc[...] += dot_nt(spread_x[:, part], lo_x[:, part])
@@ -473,7 +473,7 @@
                     depth_sum(cells), zone_lines[pl.ds(index, 1), :]
                 )
 
-        loop(cols, one)
+        loop(cols, one, 4)
         zacc[...] += dot_nt(spread_y[...], lo_y[...])
 
     def back_z(j, back):

time: 121 us -> 121 us (level)
  no operation moved by 1% of the time
where the time goes in v5:
time: 121 us
  Pallas kernels  120 us (99%)
    pallas_call x1, Pallas kernels, on_device(): pl.pallas_call(functools.partial(kernel, rows, cols, scale), out_shape=(j...  118 us

profile of v5, /device:TPU:1, one launch (start us, length us, event | category | flops | bytes accessed | tf_op | source)
XLA Modules:
  0.0 120.8 jit_solution(12035642077067852763)
XLA Ops:
  0.6 118.3 %adjoint_lines.1 = (bf16[16,128,128]{2,1,0:T(8,128)(2,1)}, f32[8,128]{1,0:T(8,128)}) custom-call(bf16[16,128,128]{2,1,0:T(8,128)(2,1)} %head_hbm.1, bf16[16,128,128]{2,1,0:T(8,128)(2,1)} %cot_hbm.1, bf16[16,128,128]{2,1,0:T(8,128)(2,1)} %cond_hbm.1, bf16[512,512]{1,0:T(8,128)(2,1)} %lx_hbm.1, bf16[1024,1024]{1,0:T(8,128)(2,1)} %ly_hbm.1, ...), custom_call_target="tpu_custom_call" | custom-call | tf_op jit(solution)/shard_map/adjoint_lines/pallas_call | solution.py:759
  118.9 1.9 %finish_slab.1 = (bf16[16,128,128]{2,1,0:T(8,128)(2,1)}, f32[8]{0:T(128)}) custom-call(bf16[16,128,128]{2,1,0:T(8,128)(2,1)} %get-tuple-element.4.slab_ref, f32[8,128]{1,0:T(8,128)} %get-tuple-element.5.zones_ref), custom_call_target="tpu_custom_call" | custom-call | tf_op jit(solution)/shard_map/finish_slab/pallas_call | solution.py:780
